TPU v7x, 256 devices: a whole 4x4x8 slice. The times are simulated.
256 devices in a mesh: ctx: 16 (over y, z_hi, core), kv: 16 (over z_lo, x).
Axes of the slice: x: 4, y: 4, z: 8 (z_hi: 2, z_lo: 4; z = z_hi * 4 + z_lo), core: 2. Of those that a mesh axis runs over, the one named last changes fastest.
Arguments:
- queries: bfloat16 [2, 3072, 8192], P(None, 'ctx', 'kv'), may hold values from -112 to 112
- key_heads: bfloat16 [3072, 1024], P('ctx'), may hold values from -14 to 14
- value_heads: bfloat16 [3072, 1024], P('ctx'), may hold values from -6 to 6
- grad_out: bfloat16 [2, 3072, 8192], P(None, 'ctx', 'kv'), may hold values from -6 to 6
- offsets: int32 [32], replicated, may hold values from 0 to 2976, as said below
Outputs:
- grad_queries: bfloat16 [2, 3072, 8192], P(None, 'ctx', 'kv')
- grad_keys: float32 [3072, 1024], P('ctx')
- grad_values: float32 [3072, 1024], P('ctx')
Inputs may be any that keep to these rules, and one draw needn't show every extreme that they name: `offsets`: each entry is a multiple of 96; every multiple below 3072 appears once; entries 2 c and 2 c + 1 sum to 2976.
All inputs are finite; a program needn't handle non-finite values.
Results may differ from a plain program's by a relative error of at most 0.0051.
Values may be sent and summed in bfloat16 or wider, within the bound.
A program may use at most 64 MiB of HBM per device.

v0:
```python
import math

import jax
import jax.numpy as jnp
from jax import lax
from jax.sharding import PartitionSpec as P

KVH = 8
HD = 128


def to_rows(tensor, head_dim):
    layer_count, token_count, full_width = tensor.shape
    shaped = tensor.reshape(layer_count, token_count, full_width // head_dim, head_dim)
    return shaped.transpose(0, 2, 1, 3).reshape(-1, head_dim)


def from_rows(tensor, layer_count, token_count, head_dim):
    heads_here = tensor.shape[0] // (layer_count * token_count)
    shaped = tensor.reshape(layer_count, heads_here, token_count, head_dim)
    return shaped.transpose(0, 2, 1, 3).reshape(layer_count, token_count, heads_here * head_dim)


def backward_rows(query_rows, grad_rows, query_pos, key_all, value_all, key_pos):
    head_dim = query_rows.shape[1]
    scale_factor = head_dim ** (-0.5)
    key_total = key_all.shape[0]
    block_len = math.gcd(key_total, 512)
    block_count = key_total // block_len
    key_blocks = key_all.reshape(block_count, block_len, head_dim)
    value_blocks = value_all.reshape(block_count, block_len, head_dim)
    pos_blocks = key_pos.reshape(block_count, block_len)
    row_count = query_rows.shape[0]

    def scores_of(key_block, pos_block):
        raw_scores = (
            jnp.einsum("rd,kd->rk", query_rows, key_block, preferred_element_type=jnp.float32)
            * scale_factor
        )
        visible = pos_block[None, :] <= query_pos[:, None]
        return (jnp.where(visible, raw_scores, -1e30), visible)

    def stats_step(running, block_data):
        running_max, running_sum = running
        key_block, pos_block = block_data
        scores, visible = scores_of(key_block, pos_block)
        new_max = jnp.maximum(running_max, jnp.max(scores, axis=1))
        weights = jnp.where(visible, jnp.exp(scores - new_max[:, None]), 0.0)
        new_sum = running_sum * jnp.exp(running_max - new_max) + jnp.sum(weights, axis=1)
        return ((new_max, new_sum), None)

    initial = (jnp.full((row_count,), -1e30, jnp.float32), jnp.zeros((row_count,), jnp.float32))
    (row_max, row_sum), ignored = lax.scan(stats_step, initial, (key_blocks, pos_blocks))

    def probability_of(scores):
        return jnp.exp(scores - row_max[:, None]) / row_sum[:, None]

    def delta_step(running, block_data):
        key_block, value_block, pos_block = block_data
        scores, visible = scores_of(key_block, pos_block)
        probability = probability_of(scores)
        grad_prob = jnp.einsum(
            "rd,kd->rk", grad_rows, value_block, preferred_element_type=jnp.float32
        )
        return (running + jnp.sum(probability * grad_prob, axis=1), None)

    row_delta, ignored = lax.scan(
        delta_step, jnp.zeros((row_count,), jnp.float32), (key_blocks, value_blocks, pos_blocks)
    )

    def grad_step(running, block_data):
        key_block, value_block, pos_block = block_data
        scores, visible = scores_of(key_block, pos_block)
        probability = probability_of(scores)
        grad_prob = jnp.einsum(
            "rd,kd->rk", grad_rows, value_block, preferred_element_type=jnp.float32
        )
        grad_scores = (probability * (grad_prob - row_delta[:, None])).astype(jnp.bfloat16)
        updated = running + jnp.einsum(
            "rk,kd->rd", grad_scores, key_block, preferred_element_type=jnp.float32
        )
        key_grad = (
            jnp.einsum("rk,rd->kd", grad_scores, query_rows, preferred_element_type=jnp.float32)
            * scale_factor
        )
        value_grad = jnp.einsum(
            "rk,rd->kd",
            probability.astype(jnp.bfloat16),
            grad_rows,
            preferred_element_type=jnp.float32,
        )
        return (updated, (key_grad, value_grad))

    query_acc, (key_grads, value_grads) = lax.scan(
        grad_step,
        jnp.zeros((row_count, head_dim), jnp.float32),
        (key_blocks, value_blocks, pos_blocks),
    )
    return (
        query_acc * scale_factor,
        key_grads.reshape(key_total, head_dim),
        value_grads.reshape(key_total, head_dim),
    )


def local(queries, key_heads, value_heads, grad_out, offsets):
    head_dim = HD
    sharing = lax.axis_size("kv") // KVH
    own_head = lax.axis_index("kv") // sharing
    layer_count = queries.shape[0]
    token_count = queries.shape[1]
    heads_here = queries.shape[2] // head_dim
    within = jnp.arange(token_count // 2, dtype=jnp.int32)
    all_pos = (offsets[:, None] + within[None, :]).reshape(-1)
    own_pos = lax.dynamic_slice_in_dim(all_pos, lax.axis_index("ctx") * token_count, token_count)
    key_mine = lax.dynamic_slice_in_dim(key_heads, own_head * head_dim, head_dim, 1)
    value_mine = lax.dynamic_slice_in_dim(value_heads, own_head * head_dim, head_dim, 1)
    pieces = []
    key_share = jnp.zeros((token_count, head_dim), jnp.float32)
    value_share = jnp.zeros((token_count, head_dim), jnp.float32)
    for layer_idx in range(layer_count):
        key_all, value_all = (
            lax.all_gather(key_mine, "ctx", axis=0, tiled=True),
            lax.all_gather(value_mine, "ctx", axis=0, tiled=True),
        )
        query_grad, key_part, value_part = backward_rows(
            to_rows(queries[layer_idx : layer_idx + 1], head_dim),
            to_rows(grad_out[layer_idx : layer_idx + 1], head_dim),
            jnp.tile(own_pos, heads_here),
            key_all,
            value_all,
            all_pos,
        )
        key_layer, value_layer = (
            lax.psum_scatter(key_part, "ctx", scatter_dimension=0, tiled=True),
            lax.psum_scatter(value_part, "ctx", scatter_dimension=0, tiled=True),
        )
        key_share = key_share + key_layer
        value_share = value_share + value_layer
        pieces.append(from_rows(query_grad.astype(jnp.bfloat16), 1, token_count, head_dim))
    grad_queries = jnp.concatenate(pieces, axis=0)
    empty = jnp.zeros((token_count, KVH * head_dim), jnp.float32)
    placed_key = lax.dynamic_update_slice_in_dim(empty, key_share, own_head * head_dim, 1)
    placed_value = lax.dynamic_update_slice_in_dim(empty, value_share, own_head * head_dim, 1)
    grad_keys, grad_values = lax.psum((placed_key, placed_value), "kv")
    return (grad_queries, grad_keys, grad_values)


def solution(mesh):
    in_specs = (P(None, "ctx", "kv"), P("ctx", None), P("ctx", None), P(None, "ctx", "kv"), P())
    out_specs = (P(None, "ctx", "kv"), P("ctx", None), P("ctx", None))
    return jax.shard_map(local, mesh=mesh, in_specs=in_specs, out_specs=out_specs, check_vma=False)
```

profile of v0, /device:TPU:8, one launch (start us, length us, event | category | flops | bytes accessed | tf_op | source)
XLA Modules:
  0.0 610.9 jit_solution(8570204417103131808)
XLA Ops:
  8.8 40.1 %all_gather.8 = bf16[3072,128]{1,0:T(8,128)(2,1)} all-gather(bf16[192,128]{1,0:T(8,128)(2,1)S(1)} %constant_dynamic-slice_fusion.7), channel_id=1, replica_groups=mesh['ctx'=16,'kv'=16] {'ctx'}, dimensions={0}, use_global_device_ids=true | all-gather | bytes 835584 | tf_op jit(solution)/shard_map/all_gather | solution.py:123
  50.1 15.1 %while.81 = (s32[]{:T(128)}, f32[768]{0:T(1024)S(1)}, f32[768]{0:T(1024)S(1)}, s32[6,512]{1,0:T(8,128)}, bf16[6,512,128]{2,1,0:T(8,128)(2,1)}, /*index=5*/bf16[7...) while((s32[]{:T(128)}, f32[768]{0:T(1024)S(1)}, f32[768]{0:T(1024)S(1)}, ...), condition=%wide.region_12.13_spmd.clone, body=%wide.region_9.12_spmd.clone.sunk | while | flops 103812864 | bytes 3537784 | solution.py:53
  66.0 32.2 %all_gather.9 = bf16[3072,128]{1,0:T(8,128)(2,1)} all-gather(bf16[192,128]{1,0:T(8,128)(2,1)S(1)} %constant_dynamic-slice_fusion.6), channel_id=1, replica_groups=mesh['ctx'=16,'kv'=16] {'ctx'}, dimensions={0}, use_global_device_ids=true | all-gather | bytes 835584 | tf_op jit(solution)/shard_map/all_gather | solution.py:124
  98.3 22.1 %while.82 = (s32[]{:T(128)}, f32[768]{0:T(1024)S(1)}, s32[6,512]{1,0:T(8,128)}, bf16[6,512,128]{2,1,0:T(8,128)(2,1)}, bf16[768,128]{1,0:T(8,128)(2,1)S(1)}, /*in...) while((s32[]{:T(128)}, f32[768]{0:T(1024)S(1)}, ...), condition=%wide.region_15.16_spmd.clone, body=%wide.region_13.15_spmd.clone.sunk | while | flops 204079872 | bytes 3838867 | solution.py:67
  100.4 1.6 fusion.179
  104.1 1.6 fusion.179
  107.8 1.6 fusion.179
  111.5 1.6 fusion.179
  115.2 1.6 fusion.179
  118.9 1.6 fusion.179
  123.0 47.6 %while.83 = (s32[]{:T(128)}, f32[768,128]{1,0:T(8,128)}, f32[6,512,128]{2,1,0:T(8,128)}, f32[6,512,128]{2,1,0:T(8,128)}, s32[6,512]{1,0:T(8,128)}, /*index=5*/bf...) while((s32[]{:T(128)}, f32[768,128]{1,0:T(8,128)}, ...), condition=%wide.region_17.18_spmd.clone, body=%wide.region_16.17_spmd.clone.sunk | while | flops 507117568 | bytes 9646119 | solution.py:94
  123.8 1.4 fusion.190
  126.6 2.1 convolution_add_fusion.5
  131.6 1.4 fusion.190
  134.4 2.2 convolution_add_fusion.5
  139.6 1.4 fusion.190
  142.3 2.2 convolution_add_fusion.5
  147.6 1.4 fusion.190
  150.3 2.2 convolution_add_fusion.5
  155.5 1.4 fusion.190
  158.2 2.2 convolution_add_fusion.5
  163.5 1.4 fusion.190
  166.2 2.2 convolution_add_fusion.5
  170.6 18.5 %while.78 = (s32[]{:T(128)}, f32[768]{0:T(1024)S(1)}, f32[768]{0:T(1024)}, s32[6,512]{1,0:T(8,128)}, bf16[6,512,128]{2,1,0:T(8,128)(2,1)}, /*index=5*/bf16[768,1...) while((s32[]{:T(128)}, f32[768]{0:T(1024)S(1)}, f32[768]{0:T(1024)}, ...), condition=%wide.region_3.4_spmd.clone, body=%wide.region_0.3_spmd.clone.sunk | while | flops 103812864 | bytes 3562416 | solution.py:53
  189.1 22.2 %while.79 = (s32[]{:T(128)}, f32[768]{0:T(1024)S(1)}, s32[6,512]{1,0:T(8,128)}, bf16[6,512,128]{2,1,0:T(8,128)(2,1)}, bf16[768,128]{1,0:T(8,128)(2,1)S(1)}, /*in...) while((s32[]{:T(128)}, f32[768]{0:T(1024)S(1)}, ...), condition=%wide.region_6.7_spmd.clone, body=%wide.region_4.6_spmd.clone.sunk | while | flops 204079872 | bytes 3851183 | solution.py:67
  191.2 1.6 fusion.155
  194.9 1.6 fusion.155
  198.6 1.6 fusion.155
  202.3 1.6 fusion.155
  206.0 1.6 fusion.155
  209.7 1.6 fusion.155
  213.9 42.6 %while.80 = (s32[]{:T(128)}, f32[768,128]{1,0:T(8,128)S(1)}, f32[6,512,128]{2,1,0:T(8,128)}, f32[6,512,128]{2,1,0:T(8,128)}, s32[6,512]{1,0:T(8,128)}, /*index=5...) while((s32[]{:T(128)}, f32[768,128]{1,0:T(8,128)S(1)}, ...), condition=%wide.region_8.9_spmd.clone, body=%wide.region_7.8_spmd.clone.sunk | while | flops 507117568 | bytes 9609179 | solution.py:94
  214.7 1.4 fusion.166
  217.4 1.4 convolution_add_fusion.4
  221.8 1.4 fusion.166
  224.5 1.4 convolution_add_fusion.4
  228.9 1.4 fusion.166
  236.0 1.4 fusion.166
  243.2 1.4 fusion.166
  245.9 1.4 convolution_add_fusion.4
  250.3 1.4 fusion.166
  253.0 1.4 convolution_add_fusion.4
  256.5 3.2 add.96
  261.2 2.7 add.97
  263.9 87.8 %reduce-scatter.3.cloned.1.call-done = f32[192,128]{1,0:T(8,128)} async-done(((f32[3072,128]{1,0:T(8,128)}), f32[192,128]{1,0:T(8,128)}) %reduce-scatter.3.cloned.1.call-update) | async-done | bytes 98320 | tf_op jit(solution)/shard_map/reduce_scatter | solution.py:135
  352.8 83.1 %reduce-scatter.5.cloned.1.call-done = f32[192,128]{1,0:T(8,128)} async-done(((f32[3072,128]{1,0:T(8,128)}), f32[192,128]{1,0:T(8,128)}) %reduce-scatter.5.cloned.1.call-update) | async-done | bytes 98320 | tf_op jit(solution)/shard_map/reduce_scatter | solution.py:136
  439.2 162.2 %all-reduce.3.cloned.1.call-done = (f32[192,1024]{1,0:T(8,128)}, f32[192,1024]{1,0:T(8,128)}) async-done(((f32[192,1024]{1,0:T(8,128)}, f32[192,1024]{1,0:T(8,128)}), (f32[192,1024]{1,0:T(8,128)}, f32[192,1024]{1,0:T(8,128)})) %all-reduce.3.cloned.1.call-update) | async-done | bytes 1572880 | tf_op jit(solution)/shard_map/psum | solution.py:145
  601.3 2.2 copy.88
  (384 shorter events, 126.9 us)
Async XLA Ops:
  7.2 1.6 copy-start
  7.2 344.6 %reduce-scatter.3.cloned.1.call-start = ((), (), s32[]{:S(2)}) async-start(), calls=%async_computation.2 | async-start | bytes 1671168 | tf_op jit(solution)/shard_map/reduce_scatter | solution.py:135
  50.1 48.1 %copy-start.9 = (bf16[2,192,512]{2,1,0:T(8,128)(2,1)S(1)}, bf16[2,192,512]{2,1,0:T(8,128)(2,1)}, u32[]{:S(2)}) copy-start(bf16[2,192,512]{2,1,0:T(8,128)(2,1)} %param.20) | copy-start | bytes 1179652
  123.0 2.3 copy-start.7
  123.0 2.3 copy-start.15
  129.7 1.1 copy-start.8
  129.7 1.1 copy-start.16
  130.8 2.3 copy-start.7
  130.8 2.3 copy-start.15
  137.7 1.1 copy-start.8
  137.7 1.1 copy-start.16
  138.8 2.3 copy-start.7
  138.8 2.3 copy-start.15
  145.6 1.1 copy-start.8
  145.6 1.1 copy-start.16
  146.7 2.3 copy-start.7
  146.7 2.3 copy-start.15
  154.7 2.3 copy-start.7
  154.7 2.3 copy-start.15
  161.6 1.1 copy-start.8
  161.6 1.1 copy-start.16
  162.6 2.3 copy-start.7
  162.6 2.3 copy-start.15
  169.5 1.1 copy-start.8
  169.5 1.1 copy-start.16
  171.4 1.7 copy-start.10
  174.5 1.7 copy-start.10
  177.6 1.7 copy-start.10
  180.7 1.7 copy-start.10
  183.8 1.7 copy-start.10
  186.8 1.7 copy-start.10
  189.1 2.1 copy-start.12
  192.8 2.1 copy-start.12
  196.5 2.1 copy-start.12
  200.2 2.1 copy-start.12
  203.9 2.1 copy-start.12
  207.6 2.1 copy-start.12
  211.3 2.6 copy-start.1
  211.4 2.5 copy-start.13
  227.0 1.1 copy-start.14
  234.2 1.1 copy-start.14
  241.3 1.1 copy-start.14
  259.7 1.4 copy-start.3
  259.8 176.1 %reduce-scatter.5.cloned.1.call-start = ((), (), s32[]{:S(2)}) async-start(), calls=%async_computation.3 | async-start | bytes 1671168 | tf_op jit(solution)/shard_map/reduce_scatter | solution.py:136
  263.9 337.4 %all-reduce.3.cloned.1.call-start = ((), (), s32[]{:S(2)}) async-start(), calls=%async_computation.4 | async-start | bytes 3145728 | tf_op jit(solution)/shard_map/psum | solution.py:145
  351.9 85.9 %copy-start.2 = (f32[768,128]{1,0:T(8,128)S(1)}, f32[768,128]{1,0:T(8,128)}, u32[]{:S(2)}) copy-start(f32[768,128]{1,0:T(8,128)} %get-tuple-element.328) | copy-start | bytes 1179652
  352.8 84.1 %copy-start.5 = (f32[192,1024]{1,0:T(8,128)}, f32[192,1024]{1,0:T(8,128)S(1)}, u32[]{:S(2)}) copy-start(f32[192,1024]{1,0:T(8,128)S(1)} %constant_dynamic-update-slice_fusion.1) | copy-start | bytes 2359300
  601.3 2.2 copy-start.6
  (12 other events, 9.8 us)
Sparse Core Ops, SparseCore 0:
  259.9 91.8 reduce-scatter.2
  355.9 79.9 reduce-scatter.4
  439.2 162.1 all-reduce.2
where the time goes:
time: 615 us; the launch traced here: 611 us
  waiting for transfers between devices  333 us (54%)
  matrix products  130 us (21%)
  blocking collectives  72.2 us (12%)
  local copies, waits for them, and re-layouts  48.3 us (8%)
  between operations  14 us (2%)
  other arithmetic  11.9 us (2%)
    psum x1, waiting for transfers between devices, local(): grad_keys, grad_values = lax.psum((placed_key, placed_value), 'kv')  162 us
    reduce_scatter x1, waiting for transfers between devices, local(): lax.psum_scatter(key_part, 'ctx', scatter_dimension=0, tiled=True)  87.8 us
    reduce_scatter x1, waiting for transfers between devices, local(): lax.psum_scatter(value_part, 'ctx', scatter_dimension=0, tiled=True)  83.1 us
    dot_general x36, matrix products, scores_of(): jnp.einsum('rd,kd->rk', query_rows, key_block, preferred_element_type=jnp...  48 us
    all_gather x1, blocking collectives, local(): lax.all_gather(key_mine, 'ctx', axis=0, tiled=True)  40.1 us
    all_gather x1, blocking collectives, local(): lax.all_gather(value_mine, 'ctx', axis=0, tiled=True)  32.2 us
    dynamic_slice x36, local copies, waits for them, and re-layouts, backward_rows(): lax.scan(stats_step, initial, (key_blocks, pos_blocks))  26 us
    dot_general x12, matrix products, grad_step(): jnp.einsum('rk,kd->rd', grad_scores, key_block, preferred_element_type=jn...  21.6 us
  transfers between devices with their start and end apart: 3, of which 3 were waited for; matrix products, arithmetic and copies ran while one was open for 1% of the time, Pallas kernels for 0%

commit v1 on v0

v1 whole, which is shorter than its diff:
```python
import jax
import jax.numpy as jnp
from jax import lax
from jax.experimental import pallas as pl
from jax.experimental.pallas import tpu as pltpu
from jax.sharding import PartitionSpec as P

KVH = 8
HD = 128
TOK = 192
HALF = 96
CTX = 16
TOTAL = CTX * TOK
BLOCKS = 2 * CTX
LAYERS = 2
HEADS = 4
ROWS = LAYERS * HEADS * HALF
TILE = 384
TILE_BLOCKS = TILE // HALF
SCALE = HD ** -0.5
EXP2_SCALE = SCALE * 1.4426950408889634
MESH = pl.DeviceIdType.MESH
BF16 = jnp.bfloat16
F32 = jnp.float32


def place():
    ctx, kv = lax.axis_index("ctx"), lax.axis_index("kv")
    return ctx // 4, (ctx // 2) % 2, ctx % 2, kv // 4, kv % 4


def ctx_of(y, z_hi, core):
    return y * 4 + z_hi * 2 + core


def head_of(z_lo, x):
    return z_lo * 2 + x // 2


def gather_kernel(k_ref, v_ref, o_ref, own_sem, send_sem, y_sem, cross_sem, chip_sem):
    y, z_hi, core, z_lo, x = place()
    kv = z_lo * 4 + x
    me = ctx_of(y, z_hi, core)
    mate = ctx_of(y, z_hi, 1 - core)
    far = 1 - z_hi
    cross_from = jnp.where(z_lo < 2, 3, 0)
    at_low, at_high = z_lo == 0, z_lo == 3

    barrier = pltpu.get_barrier_semaphore()

    def greet(ctx, kv_idx):
        pl.semaphore_signal(barrier, inc=1, device_id=(ctx, kv_idx), device_id_type=MESH)

    for step in (1, 2, 3):
        greet(ctx_of((y + step) % 4, z_hi, core), kv)
    greet(mate, kv)
    greet(ctx_of(y, far, core), cross_from * 4 + x)
    pl.semaphore_wait(barrier, jnp.where(jnp.logical_or(at_low, at_high), 6, 4))

    def head_slice(ref, head):
        return ref.at[:, pl.ds(pl.multiple_of(head * HD, HD), HD)]

    def send_input(head, slot, ctx, kv_idx, send, recv):
        copies = []
        for part, ref in enumerate((k_ref, v_ref)):
            copies.append(pltpu.make_async_remote_copy(
                src_ref=head_slice(ref, head), dst_ref=o_ref.at[slot, part], send_sem=send.at[part],
                recv_sem=recv, device_id=(ctx, kv_idx), device_id_type=MESH))
        return copies

    def unit_wait(slot, sem):
        pltpu.make_async_copy(o_ref.at[slot], o_ref.at[slot], sem).wait()

    def cross(low, act):
        for nth in range(2):
            target = 2 + nth if low else nth
            for copy in send_input(head_of(target, x), me, ctx_of(y, far, core), target * 4 + x,
                                   send_sem.at[nth], cross_sem):
                act(copy)

    @pl.when(at_low)
    def _():
        cross(True, lambda copy: copy.start())

    @pl.when(at_high)
    def _():
        cross(False, lambda copy: copy.start())

    head = head_of(z_lo, x)
    own = [pltpu.make_async_copy(head_slice(ref, head), o_ref.at[me, part], own_sem.at[part])
           for part, ref in enumerate((k_ref, v_ref))]
    for copy in own:
        copy.start()
    pending = []
    for step in (2, 1, 3):
        copies = send_input(head, me, ctx_of((y + step) % 4, z_hi, core), kv, send_sem.at[1 + step], y_sem.at[0, step - 1])
        for copy in copies:
            copy.start()
        pending += copies
    to_mate = []

    def forward(slot):
        nth = len(to_mate)
        copy = pltpu.make_async_remote_copy(
            src_ref=o_ref.at[slot], dst_ref=o_ref.at[slot], send_sem=chip_sem.at[0, nth],
            recv_sem=chip_sem.at[1, nth], device_id=(mate, kv), device_id_type=MESH)
        copy.start()
        to_mate.append(copy)

    for copy in own:
        copy.wait()
    forward(me)
    across = ctx_of(y, far, core)
    unit_wait(across, cross_sem)
    onward = []
    for step in (2, 1, 3):
        copy = pltpu.make_async_remote_copy(
            src_ref=o_ref.at[across], dst_ref=o_ref.at[across], send_sem=send_sem.at[4 + step, 0],
            recv_sem=y_sem.at[1, step - 1], device_id=(ctx_of((y + step) % 4, z_hi, core), kv), device_id_type=MESH)
        copy.start()
        onward.append(copy)
    forward(across)
    for kind, half in ((0, z_hi), (1, far)):
        for step in (1, 3, 2):
            slot = ctx_of((y - step + 4) % 4, half, core)
            unit_wait(slot, y_sem.at[kind, step - 1])
            forward(slot)
    for copy in pending + onward:
        copy.wait_send()
    for copy in to_mate:
        copy.wait()

    @pl.when(at_low)
    def _():
        cross(True, lambda copy: copy.wait_send())

    @pl.when(at_high)
    def _():
        cross(False, lambda copy: copy.wait_send())


def gather_heads(key_heads, value_heads):
    dma = pltpu.SemaphoreType.DMA
    return pl.pallas_call(
        gather_kernel,
        out_shape=jax.ShapeDtypeStruct((CTX, 2, TOK, HD), BF16),
        in_specs=[pl.BlockSpec(memory_space=pl.ANY)] * 2,
        out_specs=pl.BlockSpec(memory_space=pl.ANY),
        scratch_shapes=[dma((2,)), dma((8, 2)), dma((2, 3)), dma, dma((2, 8))],
        compiler_params=pltpu.CompilerParams(collective_id=0, has_side_effects=True),
        name="gather_heads",
    )(key_heads, value_heads)


def compute_kernel(off_ref, q_ref, g_ref, kv_ref, dq_ref, part_ref, ks, vs, qs, gs, s_scr, p_scr, dq_acc, dk_acc, dv_acc, sem):
    ctx = lax.axis_index("ctx")
    nt_dims = (((1,), (1,)), ((), ()))
    tn_dims = (((0,), (0,)), ((), ()))

    def load(block, act):
        dst = pl.ds(pl.multiple_of(off_ref[block], HALF), HALF)
        rows = pl.ds((block % 2) * HALF, HALF)
        act(pltpu.make_async_copy(kv_ref.at[block // 2, 0, rows], ks.at[dst], sem.at[0]))
        act(pltpu.make_async_copy(kv_ref.at[block // 2, 1, rows], vs.at[dst], sem.at[1]))

    for block in range(BLOCKS):
        load(block, lambda copy: copy.start())
    dk_acc[...] = jnp.zeros_like(dk_acc)
    dv_acc[...] = jnp.zeros_like(dv_acc)
    for half in range(2):
        for layer in range(LAYERS):
            for head in range(HEADS):
                unit = layer * HEADS + head
                src = (layer, slice(half * HALF, (half + 1) * HALF), slice(head * HD, (head + 1) * HD))
                qs[half, unit * HALF:(unit + 1) * HALF] = q_ref[src]
                gs[half, unit * HALF:(unit + 1) * HALF] = g_ref[src]
    pltpu.make_async_copy(ks, ks, sem.at[0]).wait()
    pltpu.make_async_copy(vs, vs, sem.at[1]).wait()

    def fold(tile, op):
        return op(tile.reshape(TILE // 8, 8, ROWS), axis=0)

    def one_half(half, _):
        start = off_ref[2 * ctx + half]
        last = start // TILE
        q_t, g_t = qs[half], gs[half]

        def scores(tile):
            return lax.dot_general(ks[pl.ds(tile * TILE, TILE)], q_t, nt_dims, preferred_element_type=F32)

        def max_step(tile, top):
            s = scores(tile)
            s_scr[pl.ds(tile * TILE, TILE)] = s
            return jnp.maximum(top, fold(s, jnp.max))

        top = lax.fori_loop(0, last, max_step, jnp.full((8, ROWS), -1e30, F32))
        s = scores(last)
        key_idx = lax.broadcasted_iota(jnp.int32, (TILE, ROWS), 0) + last * TILE
        row_idx = lax.broadcasted_iota(jnp.int32, (TILE, ROWS), 1) % HALF + start
        s = jnp.where(key_idx <= row_idx, s, -1e30)
        s_scr[pl.ds(last * TILE, TILE)] = s
        top = jnp.max(jnp.maximum(top, fold(s, jnp.max)), axis=0, keepdims=True)

        def sum_step(tile, sums):
            rows = pl.ds(tile * TILE, TILE)
            weight = jnp.exp2((s_scr[rows] - top) * EXP2_SCALE)
            grad_prob = lax.dot_general(vs[rows], g_t, nt_dims, preferred_element_type=F32)
            s_scr[rows] = weight
            p_scr[rows] = grad_prob
            return sums[0] + fold(weight, jnp.sum), sums[1] + fold(weight * grad_prob, jnp.sum)

        zero = jnp.zeros((8, ROWS), F32)
        total, delta = lax.fori_loop(0, last + 1, sum_step, (zero, zero))
        inv = 1.0 / jnp.sum(total, axis=0, keepdims=True)
        delta = jnp.sum(delta, axis=0, keepdims=True) * inv
        dq_acc[...] = jnp.zeros_like(dq_acc)

        def grad_step(tile, _):
            rows = pl.ds(tile * TILE, TILE)
            prob = s_scr[rows] * inv
            grad_scores = (prob * (p_scr[rows] - delta)).astype(BF16)
            dv_acc[rows] += jnp.dot(prob.astype(BF16), g_t, preferred_element_type=F32)
            dk_acc[rows] += jnp.dot(grad_scores, q_t, preferred_element_type=F32)
            dq_acc[...] += lax.dot_general(grad_scores, ks[rows], tn_dims, preferred_element_type=F32)
            return 0

        lax.fori_loop(0, last + 1, grad_step, 0)
        for layer in range(LAYERS):
            for head in range(HEADS):
                unit = layer * HEADS + head
                dq_ref[layer, pl.ds(pl.multiple_of(half * HALF, HALF), HALF), head * HD:(head + 1) * HD] = (
                    dq_acc[unit * HALF:(unit + 1) * HALF] * SCALE).astype(BF16)
        return 0

    lax.fori_loop(0, 2, one_half, 0)
    for block in range(BLOCKS):
        src = pl.ds(pl.multiple_of(off_ref[block], HALF), HALF)
        dst = slice((block % 2) * HALF, (block % 2 + 1) * HALF)
        part_ref[block // 2, 0, dst] = (dk_acc[src] * SCALE).astype(BF16)
        part_ref[block // 2, 1, dst] = dv_acc[src].astype(BF16)


def compute(offsets, queries, grad_out, heads):
    vmem = pl.BlockSpec(memory_space=pltpu.VMEM)
    return pl.pallas_call(
        compute_kernel,
        out_shape=(jax.ShapeDtypeStruct(queries.shape, BF16), jax.ShapeDtypeStruct((CTX, 2, TOK, HD), BF16)),
        in_specs=[pl.BlockSpec(memory_space=pltpu.SMEM), vmem, vmem, pl.BlockSpec(memory_space=pl.ANY)],
        out_specs=(vmem, vmem),
        scratch_shapes=[
            pltpu.VMEM((TOTAL, HD), BF16), pltpu.VMEM((TOTAL, HD), BF16),
            pltpu.VMEM((2, ROWS, HD), BF16), pltpu.VMEM((2, ROWS, HD), BF16),
            pltpu.VMEM((TOTAL, ROWS), F32), pltpu.VMEM((TOTAL, ROWS), F32),
            pltpu.VMEM((ROWS, HD), F32), pltpu.VMEM((TOTAL, HD), F32), pltpu.VMEM((TOTAL, HD), F32),
            pltpu.SemaphoreType.DMA((2,)),
        ],
        compiler_params=pltpu.CompilerParams(vmem_limit_bytes=56 * 1024 * 1024),
        cost_estimate=pl.CostEstimate(flops=3_400_000_000, bytes_accessed=6_000_000, transcendentals=2_600_000),
        name="attention_backward",
    )(offsets, queries, grad_out, heads)


def reduce_kernel(part_ref, o_ref, chip_in, chip_sum, y_in, y_sum, pair_in, pair_sum, far_in, chip_sem, y_sem, pair_sem, far_sem, out_sem):
    y, z_hi, core, z_lo, x = place()
    kv = z_lo * 4 + x
    me = ctx_of(y, z_hi, core)
    mate = ctx_of(y, z_hi, 1 - core)
    pair = z_lo * 4 + x + 1 - 2 * (x % 2)
    odd = x % 2

    barrier = pltpu.get_barrier_semaphore()

    def greet(ctx, kv_idx):
        pl.semaphore_signal(barrier, inc=1, device_id=(ctx, kv_idx), device_id_type=MESH)

    greet(mate, kv)
    greet(ctx_of(y, 1 - z_hi, core), kv)
    for step in (1, 2, 3):
        greet(ctx_of((y + step) % 4, z_hi, core), kv)
    for step in range(1, 16):
        greet(me, (kv + step) % 16)
    pl.semaphore_wait(barrier, 20)

    def remote(src, dst, sems, ctx, kv_idx):
        copy = pltpu.make_async_remote_copy(src_ref=src, dst_ref=dst, send_sem=sems.at[0], recv_sem=sems.at[1],
                                            device_id=(ctx, kv_idx), device_id_type=MESH)
        copy.start()
        return copy

    sent = []
    order = (2, 1, 3, 0)
    chip = []
    for step in order:
        to_y = (y + step) % 4
        for half in range(2):
            chip.append(remote(part_ref.at[ctx_of(to_y, half, 1 - core)], chip_in.at[step, half],
                               chip_sem.at[step, half], mate, kv))
    along = []
    for nth, step in enumerate(order):
        to_y = (y + step) % 4
        for half in range(2):
            chip[2 * nth + half].wait_recv()
            both = part_ref[ctx_of(to_y, half, core)].astype(F32) + chip_in[step, half].astype(F32)
            chip_sum[step, half] = both.astype(BF16)
        if step:
            along.append(remote(chip_sum.at[step], y_in.at[step - 1], y_sem.at[step - 1],
                                ctx_of(to_y, z_hi, core), kv))
    for copy in along:
        copy.wait_recv()
    y_sum[...] = (chip_sum[0].astype(F32) + y_in[0].astype(F32) + y_in[1].astype(F32) + y_in[2].astype(F32)).astype(BF16)
    across = remote(y_sum.at[:, 1 - odd], pair_in, pair_sem, me, pair)
    across.wait_recv()
    pair_sum[...] = (y_sum[:, odd].astype(F32) + pair_in[...].astype(F32)).astype(BF16)
    other = remote(pair_sum.at[1 - z_hi], far_in, far_sem, ctx_of(y, 1 - z_hi, core), kv)
    other.wait_recv()
    o_ref[kv] = (pair_sum[z_hi].astype(F32) + far_in[...].astype(F32)).astype(BF16)
    spread = []
    for step in range(1, 16):
        spread.append(remote(o_ref.at[kv], o_ref.at[kv], out_sem.at[step - 1], me, (kv + step) % 16))
    for copy in chip + along + [across, other]:
        copy.wait_send()
    for copy in spread:
        copy.wait()


def reduce_grads(parts):
    vmem = pl.BlockSpec(memory_space=pltpu.VMEM)
    dma = pltpu.SemaphoreType.DMA
    return pl.pallas_call(
        reduce_kernel,
        out_shape=jax.ShapeDtypeStruct((2 * KVH, TOK, HD), BF16),
        in_specs=[vmem],
        out_specs=vmem,
        scratch_shapes=[
            pltpu.VMEM((4, 2, 2, TOK, HD), BF16), pltpu.VMEM((4, 2, 2, TOK, HD), BF16),
            pltpu.VMEM((3, 2, 2, TOK, HD), BF16), pltpu.VMEM((2, 2, TOK, HD), BF16),
            pltpu.VMEM((2, TOK, HD), BF16), pltpu.VMEM((2, TOK, HD), BF16), pltpu.VMEM((TOK, HD), BF16),
            dma((4, 2, 2)), dma((3, 2)), dma((2,)), dma((2,)), dma((15, 2)),
        ],
        compiler_params=pltpu.CompilerParams(collective_id=1, has_side_effects=True, vmem_limit_bytes=32 * 1024 * 1024),
        name="reduce_grads",
    )(parts)


def local(queries, key_heads, value_heads, grad_out, offsets):
    heads = gather_heads(key_heads, value_heads)
    grad_queries, parts = compute(offsets, queries, grad_out, heads)
    shares = reduce_grads(parts).reshape(KVH, 2, TOK, HD)
    wide = shares.transpose(1, 2, 0, 3).reshape(2, TOK, KVH * HD).astype(F32)
    return grad_queries, wide[0], wide[1]


def solution(mesh):
    in_specs = (P(None, "ctx", "kv"), P("ctx", None), P("ctx", None), P(None, "ctx", "kv"), P())
    out_specs = (P(None, "ctx", "kv"), P("ctx", None), P("ctx", None))
    return jax.shard_map(local, mesh=mesh, in_specs=in_specs, out_specs=out_specs, check_vma=False)
```

time: 615 us -> 85.4 us (0.14)
  the two profiles are of different devices: /device:TPU:8 before, /device:TPU:38 now
where the time goes in v1:
time: 85.4 us; the launch traced here: 85.1 us
  Pallas kernels  80.4 us (94%)
  local copies, waits for them, and re-layouts  3.93 us (5%)
    pallas_call x1, Pallas kernels, reduce_grads(): pl.pallas_call(reduce_kernel, out_shape=jax.ShapeDtypeStruct((2 * KVH, TO...  43.5 us
    pallas_call x1, Pallas kernels, gather_heads(): pl.pallas_call(gather_kernel, out_shape=jax.ShapeDtypeStruct((CTX, 2, TOK...  20.8 us
    pallas_call x1, Pallas kernels, compute(): pl.pallas_call(compute_kernel, out_shape=(jax.ShapeDtypeStruct(queries.sh...  16.1 us

profile of v1, /device:TPU:38, one launch (start us, length us, event | category | flops | bytes accessed | tf_op | source)
XLA Modules:
  0.0 85.1 jit_solution(16818067329828172292)
XLA Ops:
  0.6 20.8 %gather_heads.1.kv_ref = bf16[16,2,192,128]{3,2,1,0:T(8,128)(2,1)} custom-call(bf16[192,1024]{1,0:T(8,128)(2,1)} %k_ref.1, bf16[192,1024]{1,0:T(8,128)(2,1)} %v_ref.1), custom_call_target="tpu_custom_call" | custom-call | tf_op jit(solution)/shard_map/gather_heads/pallas_call | solution.py:144
  21.4 16.1 %attention_backward.1 = (bf16[2,192,512]{2,1,0:T(8,128)(2,1)}, bf16[16,2,192,128]{3,2,1,0:T(8,128)(2,1)}) custom-call(s32[32]{0:T(128)} %off_ref.1, bf16[2,192,512]{2,1,0:T(8,128)(2,1)} %q_ref.1, bf16[2,192,512]{2,1,0:T(8,128)(2,1)} %g_ref.1, bf16[16,2,192,128]{3,2,1,0:T(8,128)(2,1)} %gather_heads.1.kv_ref), custom_call_target="tpu_custom_call" | custom-call | flops 3400000000 | bytes 6000000 | tf_op jit(solution)/shard_map/attention_backward/pallas_call | solution.py:245
  37.5 0.0 copy-start
  37.5 1.4 %copy-done = bf16[16,2,192,128]{3,2,1,0:T(8,128)(2,1)S(1)} copy-done((bf16[16,2,192,128]{3,2,1,0:T(8,128)(2,1)S(1)}, bf16[16,2,192,128]{3,2,1,0:T(8,128)(2,1)}, u32[]{:S(2)}) %copy-start) | copy-done | bytes 1572888
  38.9 43.5 %reduce_grads.1 = bf16[16,192,128]{2,1,0:T(8,128)(2,1)S(1)} custom-call(bf16[16,2,192,128]{3,2,1,0:T(8,128)(2,1)S(1)} %copy-done), custom_call_target="tpu_custom_call" | custom-call | tf_op jit(solution)/shard_map/reduce_grads/pallas_call | solution.py:329
  82.4 0.2 convert_bitcast_fusion
  82.6 0.1 fusion
  82.7 0.5 copy.9
  83.2 0.5 copy.8
  83.7 1.5 %copy_bitcast_fusion = (f32[192,1024]{1,0:T(8,128)}, f32[192,1024]{1,0:T(8,128)}) fusion(f32[24,8,8,128]{3,2,1,0:T(8,128)S(1)} %bitcast.13, f32[24,8,8,128]{3,2,1,0:T(8,128)S(1)} %bitcast.14), kind=kLoop, calls=%fused_computation.1 | loop fusion | bytes 3145728 | tf_op jit(solution)/shard_map/squeeze | solution.py:350
Async XLA Ops:
  37.5 1.4 %copy-start = (bf16[16,2,192,128]{3,2,1,0:T(8,128)(2,1)S(1)}, bf16[16,2,192,128]{3,2,1,0:T(8,128)(2,1)}, u32[]{:S(2)}) copy-start(bf16[16,2,192,128]{3,2,1,0:T(8,128)(2,1)} %get-tuple-element.6.part_ref) | copy-start | bytes 4718596

commit v2 on v0

v2 whole, which is shorter than its diff:
```python
import jax
import jax.numpy as jnp
from jax import lax
from jax.experimental import pallas as pl
from jax.experimental.pallas import tpu as pltpu
from jax.sharding import PartitionSpec as P

KVH = 8
HD = 128
TOK = 192
HALF = 96
CTX = 16
TOTAL = CTX * TOK
BLOCKS = 2 * CTX
LAYERS = 2
HEADS = 4
UNITS = LAYERS * HEADS
ROWS = UNITS * HALF
TILE = 384
TILE_BLOCKS = TILE // HALF
TILES = TOTAL // TILE
SLOTS = TILES + 1
SPLIT = 2
CHUNK = HALF // SPLIT
CHUNKS = 2 * SPLIT
SCALE = HD ** -0.5
EXP2_SCALE = SCALE * 1.4426950408889634
MESH = pl.DeviceIdType.MESH
BF16 = jnp.bfloat16
F32 = jnp.float32
KEYS, VALUES = 0, 1
RANK_OF, BLOCK_AT, TILE_OF = 0, 1, 2


def ctx_of(y, z_hi, core):
    return y * 4 + z_hi * 2 + core


def head_of(z_lo, x):
    return z_lo * 2 + x // 2


def kernel(place_ref, q_ref, g_ref, k_ref, v_ref, dq_ref, gk_ref, gv_ref,
           all_k, all_v, sorted_k, sorted_v, qs, gs, s_scr, p_scr, d_scr, k_acc, v_acc, q_acc, top_hist, sum_hist, delta_hist, stats, dq_out,
           parts, chip_in, chip_sum, y_in, y_sum, far_in, shares, grads,
           in_sem, own_sem, cross_sem, near_sem, over_sem, mate_sem, chip_sem, y_sem, far_sem, z_sem, x_sem, out_sem):
    ctx, kv = lax.axis_index("ctx"), lax.axis_index("kv")
    y, z_hi, core, z_lo, x = ctx // 4, (ctx // 2) % 2, ctx % 2, kv // 4, kv % 4
    mate = ctx_of(y, z_hi, 1 - core)
    far = ctx_of(y, 1 - z_hi, core)
    odd = x % 2
    pair = z_lo * 4 + x + 1 - 2 * odd
    y_peers = [ctx_of((y + step) % 4, z_hi, core) for step in (1, 2, 3)]
    x_peers = [z_lo * 4 + (x + step) % 4 for step in (1, 2, 3)]
    z_peers = [(z_lo + step) % 4 * 4 + x for step in (1, 2, 3)]
    at_low, at_high = z_lo == 0, z_lo == 3
    at_edge = jnp.logical_or(at_low, at_high)
    nt_dims = (((1,), (1,)), ((), ()))
    tn_dims = (((0,), (0,)), ((), ()))

    for nth, (ref, dst) in enumerate(((q_ref, qs), (g_ref, gs))):
        for half in range(2):
            for unit in range(UNITS):
                layer, head = divmod(unit, HEADS)
                pltpu.make_async_copy(
                    ref.at[layer, half * HALF:(half + 1) * HALF, head * HD:(head + 1) * HD],
                    dst.at[half, unit * HALF:(unit + 1) * HALF], in_sem.at[nth]).start()

    barrier = pltpu.get_barrier_semaphore()
    peers = [(mate, kv), (far, kv), (far, pair)] + [(c, kv) for c in y_peers] + [(ctx, k) for k in x_peers + z_peers]
    peers.append((far, jnp.where(z_lo < 2, 3, 0) * 4 + x))
    for peer in peers:
        pl.semaphore_signal(barrier, inc=1, device_id=peer, device_id_type=MESH)
    pl.semaphore_wait(barrier, jnp.where(at_edge, 14, 12))

    def describe(src, dst, send_sem, recv_sem, ctx_idx, kv_idx):
        return pltpu.make_async_remote_copy(src_ref=src, dst_ref=dst, send_sem=send_sem, recv_sem=recv_sem,
                                            device_id=(ctx_idx, kv_idx), device_id_type=MESH)

    def remote(src, dst, sems, ctx_idx, kv_idx):
        copy = describe(src, dst, sems.at[0], sems.at[1], ctx_idx, kv_idx)
        copy.start()
        return copy

    def head_slice(part, head):
        return (k_ref, v_ref)[part].at[:, :, pl.ds(pl.multiple_of(head * HD, HD), HD)]

    def tokens_of(part, ctx_idx):
        return (all_k, all_v)[part].at[pl.ds(2 * ctx_idx, 2)]

    def cross(part, act):
        for edge, targets in ((at_low, (2, 3)), (at_high, (1, 0))):
            @pl.when(edge)
            def _():
                for nth, target in enumerate(targets):
                    act(describe(head_slice(part, head_of(target, x)), tokens_of(part, ctx),
                                 cross_sem.at[part, 1 + nth], cross_sem.at[part, 0], far, target * 4 + x))

    head = head_of(z_lo, x)
    near, over, to_mate = {}, {}, {}

    def send_near(part):
        near[part] = [remote(head_slice(part, head), tokens_of(part, ctx), near_sem.at[part, step - 1], y_peers[step - 1], kv)
                      for step in (1, 2, 3)]

    def send_over(part):
        pltpu.make_async_copy(tokens_of(part, far), tokens_of(part, far), cross_sem.at[part, 0]).wait()
        over[part] = [remote(tokens_of(part, far), tokens_of(part, far), over_sem.at[part, step - 1], y_peers[step - 1], kv)
                      for step in (1, 2, 3)]

    def send_mate(part, step, half):
        idx = ctx_of((y - step + 4) % 4, half, core)
        to_mate.setdefault(part, []).append(
            remote(tokens_of(part, idx), tokens_of(part, idx), mate_sem.at[part, len(to_mate.get(part, []))], mate, kv))

    own = [pltpu.make_async_copy(head_slice(part, head), tokens_of(part, ctx), own_sem.at[part]) for part in (KEYS, VALUES)]
    cross(KEYS, lambda copy: copy.start())
    send_near(KEYS)
    for copy in own:
        copy.start()
    cross(KEYS, lambda copy: copy.wait_send())
    cross(VALUES, lambda copy: copy.start())
    own[KEYS].wait()
    send_mate(KEYS, 0, z_hi)
    send_over(KEYS)
    send_mate(KEYS, 0, 1 - z_hi)
    for step in (1, 3, 2):
        near[KEYS][step - 1].wait_recv()
        send_mate(KEYS, step, z_hi)
    send_near(VALUES)
    own[VALUES].wait()
    send_mate(VALUES, 0, z_hi)
    for step in (1, 3, 2):
        over[KEYS][step - 1].wait_recv()
        send_mate(KEYS, step, 1 - z_hi)
    send_over(VALUES)
    send_mate(VALUES, 0, 1 - z_hi)
    for copy in to_mate[KEYS]:
        copy.wait_recv()

    def sort(part):
        for rank in range(BLOCKS):
            first = rank % TILE_BLOCKS * HALF
            (sorted_k, sorted_v)[part][rank // TILE_BLOCKS, first:first + HALF] = (all_k, all_v)[part][place_ref[BLOCK_AT, rank]]

    sort(KEYS)
    pltpu.make_async_copy(qs, qs, in_sem.at[0]).wait()
    pltpu.make_async_copy(gs, gs, in_sem.at[1]).wait()

    start_0, start_1 = place_ref[RANK_OF, 2 * ctx] * HALF, place_ref[RANK_OF, 2 * ctx + 1] * HALF
    count_0 = place_ref[TILE_OF, 2 * ctx] + 1
    count_1 = SLOTS - count_0

    def slot_of(slot):
        half = (slot >= count_0).astype(jnp.int32)
        tile = slot - count_0 * half
        return half, tile, tile, pl.ds(pl.multiple_of(slot * TILE, TILE), TILE)

    def carried(slot):
        return (slot != count_0).astype(F32)

    def fold(tile, op):
        return op(tile.reshape(TILE // 8, 8, ROWS), axis=0)

    def score_step(slot, top):
        half, tile, keys, rows = slot_of(slot)
        s = lax.dot_general(sorted_k[keys], qs[half], nt_dims, preferred_element_type=F32)
        ahead = lax.broadcasted_iota(jnp.int32, (TILE, ROWS), 0) - lax.broadcasted_iota(jnp.int32, (TILE, ROWS), 1) % HALF
        s = jnp.where(ahead <= start_0 + (start_1 - start_0) * half - tile * TILE, s, -1e30)
        s_scr[rows] = s
        keep = carried(slot)
        top = jnp.maximum(top * keep - 1e30 * (1.0 - keep), fold(s, jnp.max))
        top_hist[slot] = top
        return top

    top = lax.fori_loop(0, 4, score_step, jnp.full((8, ROWS), -1e30, F32))
    for step in (1, 3, 2):
        near[VALUES][step - 1].wait_recv()
        send_mate(VALUES, step, z_hi)
    for step in (1, 3, 2):
        over[VALUES][step - 1].wait_recv()
        send_mate(VALUES, step, 1 - z_hi)
    lax.fori_loop(4, SLOTS, score_step, top)
    for half, last in enumerate((count_0 - 1, SLOTS - 1)):
        stats[half, 0] = jnp.broadcast_to(jnp.max(top_hist[last], axis=0, keepdims=True), (8, ROWS))
    for copy in to_mate[VALUES]:
        copy.wait_recv()
    sort(VALUES)

    def sum_step(slot, sums):
        half, tile, keys, rows = slot_of(slot)
        weight = jnp.exp2((s_scr[rows] - stats[half, 0][:1]) * EXP2_SCALE)
        grad_prob = lax.dot_general(sorted_v[keys], gs[half], nt_dims, preferred_element_type=F32)
        s_scr[rows] = weight
        p_scr[rows] = grad_prob
        keep = carried(slot)
        total, delta = sums[0] * keep + fold(weight, jnp.sum), sums[1] * keep + fold(weight * grad_prob, jnp.sum)
        sum_hist[slot], delta_hist[slot] = total, delta
        return total, delta

    zero = jnp.zeros((8, ROWS), F32)
    lax.fori_loop(0, SLOTS, sum_step, (zero, zero))
    for half, last in enumerate((count_0 - 1, SLOTS - 1)):
        inv = 1.0 / jnp.sum(sum_hist[last], axis=0, keepdims=True)
        delta = jnp.sum(delta_hist[last], axis=0, keepdims=True) * inv
        stats[half, 1] = jnp.broadcast_to(inv, (8, ROWS))
        stats[half, 2] = jnp.broadcast_to(delta, (8, ROWS))

    def value_step(slot, _):
        half, tile, keys, rows = slot_of(slot)
        prob = s_scr[rows] * stats[half, 1][:1]
        v_acc[pl.ds(slot * TILE_BLOCKS, TILE_BLOCKS)] = jnp.dot(prob.astype(BF16), gs[half], preferred_element_type=F32).reshape(TILE_BLOCKS, HALF, HD)
        d_scr[rows] = (prob * (p_scr[rows] - stats[half, 2][:1])).astype(BF16)
        return 0

    def key_step(slot, _):
        half, tile, keys, rows = slot_of(slot)
        k_acc[pl.ds(slot * TILE_BLOCKS, TILE_BLOCKS)] = jnp.dot(d_scr[rows], qs[half], preferred_element_type=F32).reshape(TILE_BLOCKS, HALF, HD)
        return 0

    def query_step(slot, _):
        half, tile, keys, rows = slot_of(slot)
        term = lax.dot_general(d_scr[rows], sorted_k[keys], tn_dims, preferred_element_type=F32)
        q_acc[slot] = term + q_acc[jnp.maximum(slot - 1, 0)] * carried(slot)
        return 0

    def by_tokens(part, acc, scale):
        for block in range(BLOCKS):
            rank = place_ref[RANK_OF, block]
            in_0 = (rank < count_0 * TILE_BLOCKS).astype(jnp.int32)
            in_1 = (rank < count_1 * TILE_BLOCKS).astype(jnp.int32)
            both = (acc[rank * in_0] * (in_0.astype(F32) * scale)
                    + acc[(count_0 * TILE_BLOCKS + rank) * in_1] * (in_1.astype(F32) * scale))
            parts[part, block // 2 % 2, block // 8, block // 4 % 2, block % 2] = both.astype(BF16)

    chunks = {VALUES: range(SPLIT), KEYS: range(SPLIT, CHUNKS)}
    chip, along, across, along_z, along_x = {}, {}, {}, {}, {}

    def rows_of(chunk):
        return slice(chunk % SPLIT * CHUNK, (chunk % SPLIT + 1) * CHUNK)

    def send_chip(part):
        for chunk in chunks[part]:
            chip[chunk] = remote(parts.at[part, 1 - core, :, :, :, rows_of(chunk)], chip_in.at[chunk], chip_sem.at[chunk], mate, kv)

    def send_y(part):
        for chunk in chunks[part]:
            chip[chunk].wait_recv()
            along[chunk] = []
            for step in (2, 1, 3, 0):
                to_y = (y + step) % 4
                both = parts[part, core, to_y, :, :, rows_of(chunk)].astype(F32) + chip_in[chunk, to_y].astype(F32)
                chip_sum[chunk, step] = both.astype(BF16)
                if step:
                    along[chunk].append(remote(chip_sum.at[chunk, step], y_in.at[chunk, step - 1],
                                               y_sem.at[chunk, step - 1], y_peers[step - 1], kv))

    def send_far(part):
        for chunk in chunks[part]:
            for copy in along[chunk]:
                copy.wait_recv()
            total = chip_sum[chunk, 0].astype(F32)
            for step in range(3):
                total += y_in[chunk, step].astype(F32)
            y_sum[chunk] = total.astype(BF16)
            across[chunk] = [
                remote(y_sum.at[chunk, 1 - z_hi, 1 - odd], far_in.at[chunk, 0], far_sem.at[chunk, 0], far, pair),
                remote(y_sum.at[chunk, 1 - z_hi, odd], far_in.at[chunk, 1], far_sem.at[chunk, 1], far, kv),
                remote(y_sum.at[chunk, z_hi, 1 - odd], far_in.at[chunk, 2], far_sem.at[chunk, 2], ctx, pair)]

    def send_x(chunk, z_step):
        slot = shares.at[chunk, x, (z_lo - z_step + 4) % 4]
        along_x.setdefault(chunk, []).extend(
            remote(slot, slot, x_sem.at[chunk, z_step, step - 1], ctx, x_peers[step - 1]) for step in (2, 1, 3))

    def send_z(part):
        for chunk in chunks[part]:
            for copy in across[chunk]:
                copy.wait_recv()
            total = y_sum[chunk, z_hi, odd].astype(F32)
            for nth in range(3):
                total += far_in[chunk, nth].astype(F32)
            shares[chunk, x, z_lo] = total.astype(BF16)
            slot = shares.at[chunk, x, z_lo]
            along_z[chunk] = [remote(slot, slot, z_sem.at[chunk, step - 1], ctx, z_peers[step - 1]) for step in (1, 2, 3)]
            send_x(chunk, 0)

    def pass_on(part):
        for chunk in chunks[part]:
            for z_step in (1, 2, 3):
                along_z[chunk][z_step - 1].wait_recv()
                send_x(chunk, z_step)

    def finish(part):
        for chunk in chunks[part]:
            for copy in along_x[chunk]:
                copy.wait_recv()
            rows = rows_of(chunk)
            for z_idx in range(4):
                for x_idx in range(4):
                    first = (x_idx % 2) * HALF
                    col = head_of(z_idx, x_idx) * HD
                    grads[part, first + rows.start:first + rows.stop, col:col + HD] = shares[chunk, x_idx, z_idx].astype(F32)
        copy = pltpu.make_async_copy(grads.at[part], (gk_ref, gv_ref)[part], out_sem.at[part])
        copy.start()
        return copy

    lax.fori_loop(0, SLOTS, value_step, 0)
    by_tokens(VALUES, v_acc, 1.0)
    send_chip(VALUES)
    lax.fori_loop(0, SLOTS, key_step, 0)
    send_y(VALUES)
    by_tokens(KEYS, k_acc, SCALE)
    send_chip(KEYS)
    q_acc[0] = jnp.zeros((ROWS, HD), F32)
    lax.fori_loop(0, 4, query_step, 0)
    send_y(KEYS)
    lax.fori_loop(4, SLOTS, query_step, 0)
    send_far(VALUES)
    for half in range(2):
        last = count_0 - 1 if half == 0 else SLOTS - 1
        for unit in range(UNITS):
            layer, head_idx = divmod(unit, HEADS)
            dq_out[layer, half * HALF:(half + 1) * HALF, head_idx * HD:(head_idx + 1) * HD] = (
                q_acc[last, unit * HALF:(unit + 1) * HALF] * SCALE).astype(BF16)
    dq_copy = pltpu.make_async_copy(dq_out, dq_ref, out_sem.at[2])
    dq_copy.start()
    send_far(KEYS)
    send_z(VALUES)
    send_z(KEYS)
    pass_on(VALUES)
    pass_on(KEYS)
    written = [dq_copy, finish(VALUES), finish(KEYS)]
    for copy in written:
        copy.wait()
    cross(VALUES, lambda copy: copy.wait_send())
    for group in (near, over, to_mate, along, across, along_z, along_x):
        for copies in group.values():
            for copy in copies:
                copy.wait_send()
    for copy in chip.values():
        copy.wait_send()


def local(queries, key_heads, value_heads, grad_out, offsets):
    ranks = jnp.arange(BLOCKS, dtype=jnp.int32)
    blocks = jnp.sum(jnp.where(offsets[None, :] == ranks[:, None] * HALF, ranks[None, :], 0), axis=1)
    places = jnp.stack([offsets // HALF, blocks, offsets // TILE])
    dma, vmem = pltpu.SemaphoreType.DMA, pltpu.VMEM
    hbm = pl.BlockSpec(memory_space=pl.ANY)
    smem = pl.BlockSpec(memory_space=pltpu.SMEM)
    grads = jax.ShapeDtypeStruct((TOK, KVH * HD), F32)
    return pl.pallas_call(
        kernel,
        out_shape=(jax.ShapeDtypeStruct(queries.shape, BF16), grads, grads),
        in_specs=[smem, hbm, hbm, hbm, hbm],
        out_specs=(hbm, hbm, hbm),
        scratch_shapes=[
            vmem((BLOCKS, HALF, HD), BF16), vmem((BLOCKS, HALF, HD), BF16), vmem((TILES, TILE, HD), BF16), vmem((TILES, TILE, HD), BF16),
            vmem((2, ROWS, HD), BF16), vmem((2, ROWS, HD), BF16),
            vmem((SLOTS * TILE, ROWS), F32), vmem((SLOTS * TILE, ROWS), F32), vmem((SLOTS * TILE, ROWS), BF16),
            vmem((SLOTS * TILE_BLOCKS, HALF, HD), F32), vmem((SLOTS * TILE_BLOCKS, HALF, HD), F32), vmem((SLOTS, ROWS, HD), F32),
            vmem((SLOTS, 8, ROWS), F32), vmem((SLOTS, 8, ROWS), F32), vmem((SLOTS, 8, ROWS), F32), vmem((2, 3, 8, ROWS), F32),
            vmem((LAYERS, TOK, HEADS * HD), BF16),
            vmem((2, 2, 4, 2, 2, HALF, HD), BF16),
            vmem((CHUNKS, 4, 2, 2, CHUNK, HD), BF16), vmem((CHUNKS, 4, 2, 2, CHUNK, HD), BF16),
            vmem((CHUNKS, 3, 2, 2, CHUNK, HD), BF16), vmem((CHUNKS, 2, 2, CHUNK, HD), BF16),
            vmem((CHUNKS, 3, CHUNK, HD), BF16), vmem((CHUNKS, 4, 4, CHUNK, HD), BF16),
            vmem((2, TOK, KVH * HD), F32),
            dma((2,)), dma((2,)), dma((2, 3)), dma((2, 3, 2)), dma((2, 3, 2)), dma((2, 8, 2)),
            dma((CHUNKS, 2)), dma((CHUNKS, 3, 2)), dma((CHUNKS, 3, 2)), dma((CHUNKS, 3, 2)), dma((CHUNKS, 4, 3, 2)), dma((3,)),
        ],
        compiler_params=pltpu.CompilerParams(collective_id=0, has_side_effects=True, vmem_limit_bytes=58 * 1024 * 1024),
        cost_estimate=pl.CostEstimate(flops=3_400_000_000, bytes_accessed=6_000_000, transcendentals=2_600_000),
        name="attention_backward",
    )(places, queries, grad_out, key_heads.reshape(2, HALF, KVH * HD), value_heads.reshape(2, HALF, KVH * HD))


def solution(mesh):
    in_specs = (P(None, "ctx", "kv"), P("ctx", None), P("ctx", None), P(None, "ctx", "kv"), P())
    out_specs = (P(None, "ctx", "kv"), P("ctx", None), P("ctx", None))
    return jax.shard_map(local, mesh=mesh, in_specs=in_specs, out_specs=out_specs, check_vma=False)
```

time: 615 us -> 68.1 us (0.11)
  waiting for transfers between devices: 333 us -> 0 us
  matrix products: 130 us -> 0 us
  blocking collectives: 72.2 us -> 0 us
  Pallas kernels: 0 us -> 61.6 us
  local copies, waits for them, and re-layouts: 48.3 us -> 4.78 us
  between operations: 14 us -> 0.67 us
  other arithmetic: 11.9 us -> 0.78 us
    reduce_scatter x2 -> x0, waiting for transfers between devices: 171 us -> none  [the longest x1 87.8 us: local(): lax.psum_scatter(key_part, 'ctx', scatter_dimension=0, tiled=True)]
    psum x1 -> x0, waiting for transfers between devices: 162 us -> none  [local(): grad_keys, grad_values = lax.psum((placed_key, placed_value), 'kv')]
    dot_general x96 -> x0, matrix products: 130 us -> none  [the longest x36 48 us: scores_of(): jnp.einsum('rd,kd->rk', query_rows, key_block, preferred_element_type=jnp...]
    all_gather x2 -> x0, blocking collectives: 72.2 us -> none  [the longest x1 40.1 us: local(): lax.all_gather(key_mine, 'ctx', axis=0, tiled=True)]
    pallas_call x0 -> x1, Pallas kernels: none -> 61.6 us  [local(): pl.pallas_call(kernel, out_shape=(jax.ShapeDtypeStruct(queries.shape, BF1...]
    dynamic_slice x39 -> x0, local copies, waits for them, and re-layouts: 27 us -> none  [the longest x36 26 us: backward_rows(): lax.scan(stats_step, initial, (key_blocks, pos_blocks))]
    add x27 -> x0, other arithmetic: 6.88 us -> none  [the longest x1 3.2 us: local(): key_share = key_share + key_layer]
  transfers between devices with their start and end apart: 3 -> 0, of which waited for: 3 -> 0; matrix products, arithmetic and copies ran while one was open for 1% -> 0% of each run, Pallas kernels for 0% -> 0%
where the time goes in v2:
time: 68.1 us; the launch traced here: 67.9 us
  Pallas kernels  61.6 us (90%)
  local copies, waits for them, and re-layouts  4.78 us (7%)
  other arithmetic  0.78 us (1%)
    pallas_call x1, Pallas kernels, local(): pl.pallas_call(kernel, out_shape=(jax.ShapeDtypeStruct(queries.shape, BF1...  61.6 us
    unnamed x9, local copies, waits for them, and re-layouts  4.78 us

profile of v2, /device:TPU:8, one launch (start us, length us, event | category | flops | bytes accessed | tf_op | source)
XLA Modules:
  0.0 67.9 jit_solution(16468477089291576427)
XLA Ops:
  0.6 0.0 copy-start.2
  0.7 0.6 copy-done.2
  1.3 0.2 select_reduce_fusion
  1.5 0.6 pad_add_fusion.place_ref
  2.1 61.6 %attention_backward.1 = (bf16[2,192,512]{2,1,0:T(8,128)(2,1)}, f32[192,1024]{1,0:T(8,128)}, f32[192,1024]{1,0:T(8,128)}) custom-call(s32[3,32]{1,0:T(4,128)} %pad_add_fusion.place_ref, bf16[2,192,512]{2,1,0:T(8,128)(2,1)} %q_ref.1, bf16[2,192,512]{2,1,0:T(8,128)(2,1)} %g_ref.1, bf16[2,96,1024]{2,1,0:T(8,128)(2,1)} %bitcast.8, bf16[2,96,1024]{2,1,0:T(8,128)(2,1)} %bitcast.9), custom_call_target="tpu_custom_call" | custom-call | flops 3400000000 | bytes 6000000 | tf_op jit(solution)/shard_map/attention_backward/pallas_call | solution.py:353
  63.7 0.0 copy-start.1
  63.7 1.8 %copy.11 = bf16[2,192,512]{2,1,0:T(8,128)(2,1)} copy(bf16[2,192,512]{2,1,0:T(8,128)(2,1)} %get-tuple-element.8) | data formatting | bytes 786432
  65.6 0.0 copy-done.1
  65.6 0.0 copy-start
  65.6 0.9 %copy.12 = f32[192,1024]{1,0:T(8,128)} copy(f32[192,1024]{1,0:T(8,128)S(1)} %copy-done.1) | data formatting | bytes 1572864
  66.4 0.5 copy-done
  67.0 0.9 %copy.13 = f32[192,1024]{1,0:T(8,128)} copy(f32[192,1024]{1,0:T(8,128)S(1)} %copy-done) | data formatting | bytes 1572864
  (2 shorter events, 0.0 us)
Async XLA Ops:
  0.6 0.7 copy-start.2
  63.7 1.9 %copy-start.1 = (f32[192,1024]{1,0:T(8,128)S(1)}, f32[192,1024]{1,0:T(8,128)}, u32[]{:S(2)}) copy-start(f32[192,1024]{1,0:T(8,128)} %get-tuple-element.9) | copy-start | bytes 2359300
  65.6 1.4 %copy-start = (f32[192,1024]{1,0:T(8,128)S(1)}, f32[192,1024]{1,0:T(8,128)}, u32[]{:S(2)}) copy-start(f32[192,1024]{1,0:T(8,128)} %get-tuple-element.10) | copy-start | bytes 2359300

commit v3 on v2

--- a/solution.py
+++ b/solution.py
@@ -28,6 +28,7 @@
 MESH = pl.DeviceIdType.MESH
 BF16 = jnp.bfloat16
 F32 = jnp.float32
+UNROLL = 3
 KEYS, VALUES = 0, 1
 RANK_OF, BLOCK_AT, TILE_OF = 0, 1, 2
 
@@ -40,10 +41,10 @@
     return z_lo * 2 + x // 2
 
 
-def kernel(place_ref, q_ref, g_ref, k_ref, v_ref, dq_ref, gk_ref, gv_ref,
+def kernel(place_ref, q_ref, g_ref, k_ref, v_ref, dq_ref, out_ref,
            all_k, all_v, sorted_k, sorted_v, qs, gs, s_scr, p_scr, d_scr, k_acc, v_acc, q_acc, top_hist, sum_hist, delta_hist, stats, dq_out,
-           parts, chip_in, chip_sum, y_in, y_sum, far_in, shares, grads,
-           in_sem, own_sem, cross_sem, near_sem, over_sem, mate_sem, chip_sem, y_sem, far_sem, z_sem, x_sem, out_sem):
+           parts, chip_in, chip_sum, y_in, y_sum, z_in, shares,
+           in_sem, own_sem, cross_sem, near_sem, over_sem, mate_sem, chip_sem, y_sem, z_sem, x_sem, out_sem):
     ctx, kv = lax.axis_index("ctx"), lax.axis_index("kv")
     y, z_hi, core, z_lo, x = ctx // 4, (ctx // 2) % 2, ctx % 2, kv // 4, kv % 4
     mate = ctx_of(y, z_hi, 1 - core)
@@ -54,7 +55,6 @@
     x_peers = [z_lo * 4 + (x + step) % 4 for step in (1, 2, 3)]
     z_peers = [(z_lo + step) % 4 * 4 + x for step in (1, 2, 3)]
     at_low, at_high = z_lo == 0, z_lo == 3
-    at_edge = jnp.logical_or(at_low, at_high)
     nt_dims = (((1,), (1,)), ((), ()))
     tn_dims = (((0,), (0,)), ((), ()))
 
@@ -67,11 +67,11 @@
                     dst.at[half, unit * HALF:(unit + 1) * HALF], in_sem.at[nth]).start()
 
     barrier = pltpu.get_barrier_semaphore()
-    peers = [(mate, kv), (far, kv), (far, pair)] + [(c, kv) for c in y_peers] + [(ctx, k) for k in x_peers + z_peers]
-    peers.append((far, jnp.where(z_lo < 2, 3, 0) * 4 + x))
+    peers = [(mate, kv)] + [(c, k) for c in y_peers for k in (kv, pair)] + [(ctx, k) for k in x_peers + z_peers]
+    peers += [(far, z_idx * 4 + x) for z_idx in range(4)]
     for peer in peers:
         pl.semaphore_signal(barrier, inc=1, device_id=peer, device_id_type=MESH)
-    pl.semaphore_wait(barrier, jnp.where(at_edge, 14, 12))
+    pl.semaphore_wait(barrier, len(peers))
 
     def describe(src, dst, send_sem, recv_sem, ctx_idx, kv_idx):
         return pltpu.make_async_remote_copy(src_ref=src, dst_ref=dst, send_sem=send_sem, recv_sem=recv_sem,
@@ -122,19 +122,24 @@
     cross(VALUES, lambda copy: copy.start())
     own[KEYS].wait()
     send_mate(KEYS, 0, z_hi)
+    for copy in near[KEYS]:
+        copy.wait_send()
+    send_near(VALUES)
+    own[VALUES].wait()
+    send_mate(VALUES, 0, z_hi)
     send_over(KEYS)
     send_mate(KEYS, 0, 1 - z_hi)
     for step in (1, 3, 2):
         near[KEYS][step - 1].wait_recv()
         send_mate(KEYS, step, z_hi)
-    send_near(VALUES)
-    own[VALUES].wait()
-    send_mate(VALUES, 0, z_hi)
+    send_over(VALUES)
+    send_mate(VALUES, 0, 1 - z_hi)
     for step in (1, 3, 2):
         over[KEYS][step - 1].wait_recv()
         send_mate(KEYS, step, 1 - z_hi)
-    send_over(VALUES)
-    send_mate(VALUES, 0, 1 - z_hi)
+    for step in (1, 3, 2):
+        near[VALUES][step - 1].wait_recv()
+        send_mate(VALUES, step, z_hi)
     for copy in to_mate[KEYS]:
         copy.wait_recv()
 
@@ -173,14 +178,11 @@
         top_hist[slot] = top
         return top
 
-    top = lax.fori_loop(0, 4, score_step, jnp.full((8, ROWS), -1e30, F32))
-    for step in (1, 3, 2):
-        near[VALUES][step - 1].wait_recv()
-        send_mate(VALUES, step, z_hi)
+    top = lax.fori_loop(0, SLOTS - UNROLL, score_step, jnp.full((8, ROWS), -1e30, F32), unroll=UNROLL)
     for step in (1, 3, 2):
         over[VALUES][step - 1].wait_recv()
         send_mate(VALUES, step, 1 - z_hi)
-    lax.fori_loop(4, SLOTS, score_step, top)
+    lax.fori_loop(SLOTS - UNROLL, SLOTS, score_step, top, unroll=UNROLL)
     for half, last in enumerate((count_0 - 1, SLOTS - 1)):
         stats[half, 0] = jnp.broadcast_to(jnp.max(top_hist[last], axis=0, keepdims=True), (8, ROWS))
     for copy in to_mate[VALUES]:
@@ -199,7 +201,7 @@
         return total, delta
 
     zero = jnp.zeros((8, ROWS), F32)
-    lax.fori_loop(0, SLOTS, sum_step, (zero, zero))
+    lax.fori_loop(0, SLOTS, sum_step, (zero, zero), unroll=UNROLL)
     for half, last in enumerate((count_0 - 1, SLOTS - 1)):
         inv = 1.0 / jnp.sum(sum_hist[last], axis=0, keepdims=True)
         delta = jnp.sum(delta_hist[last], axis=0, keepdims=True) * inv
@@ -231,10 +233,10 @@
             in_1 = (rank < count_1 * TILE_BLOCKS).astype(jnp.int32)
             both = (acc[rank * in_0] * (in_0.astype(F32) * scale)
                     + acc[(count_0 * TILE_BLOCKS + rank) * in_1] * (in_1.astype(F32) * scale))
-            parts[part, block // 2 % 2, block // 8, block // 4 % 2, block % 2] = both.astype(BF16)
-
-    chunks = {VALUES: range(SPLIT), KEYS: range(SPLIT, CHUNKS)}
-    chip, along, across, along_z, along_x = {}, {}, {}, {}, {}
+            parts[part, block // 2 % 2, block // 8, block % 2, block // 4 % 2] = both.astype(BF16)
+
+    chunks = {KEYS: range(SPLIT), VALUES: range(SPLIT, CHUNKS)}
+    chip, along, along_z, along_x = {}, {}, {}, {}
 
     def rows_of(chunk):
         return slice(chunk % SPLIT * CHUNK, (chunk % SPLIT + 1) * CHUNK)
@@ -251,64 +253,49 @@
                 to_y = (y + step) % 4
                 both = parts[part, core, to_y, :, :, rows_of(chunk)].astype(F32) + chip_in[chunk, to_y].astype(F32)
                 chip_sum[chunk, step] = both.astype(BF16)
-                if step:
-                    along[chunk].append(remote(chip_sum.at[chunk, step], y_in.at[chunk, step - 1],
-                                               y_sem.at[chunk, step - 1], y_peers[step - 1], kv))
-
-    def send_far(part):
+                to_ctx = y_peers[step - 1] if step else ctx
+                for other in ((1, 0) if step else (1,)):
+                    nth = 2 * step + other - 1
+                    along[chunk].append(remote(chip_sum.at[chunk, step, 1 - odd if other else odd], y_in.at[chunk, nth],
+                                               y_sem.at[chunk, nth], to_ctx, pair if other else kv))
+
+    def send_z(part):
         for chunk in chunks[part]:
             for copy in along[chunk]:
                 copy.wait_recv()
-            total = chip_sum[chunk, 0].astype(F32)
-            for step in range(3):
-                total += y_in[chunk, step].astype(F32)
+            total = chip_sum[chunk, 0, odd].astype(F32)
+            for nth in range(7):
+                total += y_in[chunk, nth].astype(F32)
             y_sum[chunk] = total.astype(BF16)
-            across[chunk] = [
-                remote(y_sum.at[chunk, 1 - z_hi, 1 - odd], far_in.at[chunk, 0], far_sem.at[chunk, 0], far, pair),
-                remote(y_sum.at[chunk, 1 - z_hi, odd], far_in.at[chunk, 1], far_sem.at[chunk, 1], far, kv),
-                remote(y_sum.at[chunk, z_hi, 1 - odd], far_in.at[chunk, 2], far_sem.at[chunk, 2], ctx, pair)]
-
-    def send_x(chunk, z_step):
-        slot = shares.at[chunk, x, (z_lo - z_step + 4) % 4]
-        along_x.setdefault(chunk, []).extend(
-            remote(slot, slot, x_sem.at[chunk, z_step, step - 1], ctx, x_peers[step - 1]) for step in (2, 1, 3))
-
-    def send_z(part):
+            along_z[chunk] = [
+                remote(y_sum.at[chunk, 1 - z_hi], z_in.at[chunk, 1, z_lo], z_sem.at[chunk, 1, step], far, (z_lo + step) % 4 * 4 + x)
+                for step in (0, 3, 1, 2)]
+            along_z[chunk] += [
+                remote(y_sum.at[chunk, z_hi], z_in.at[chunk, 0, z_lo], z_sem.at[chunk, 0, step], ctx, z_peers[step - 1])
+                for step in (3, 2, 1)]
+            z_in[chunk, 0, z_lo] = y_sum[chunk, z_hi]
+
+    def send_x(part):
         for chunk in chunks[part]:
-            for copy in across[chunk]:
+            for copy in along_z[chunk]:
                 copy.wait_recv()
-            total = y_sum[chunk, z_hi, odd].astype(F32)
-            for nth in range(3):
-                total += far_in[chunk, nth].astype(F32)
-            shares[chunk, x, z_lo] = total.astype(BF16)
-            slot = shares.at[chunk, x, z_lo]
-            along_z[chunk] = [remote(slot, slot, z_sem.at[chunk, step - 1], ctx, z_peers[step - 1]) for step in (1, 2, 3)]
-            send_x(chunk, 0)
-
-    def pass_on(part):
-        for chunk in chunks[part]:
-            for z_step in (1, 2, 3):
-                along_z[chunk][z_step - 1].wait_recv()
-                send_x(chunk, z_step)
+            shares[chunk, x] = (z_in[chunk, 0].astype(F32) + z_in[chunk, 1].astype(F32)).astype(BF16)
+            slot = shares.at[chunk, x]
+            along_x[chunk] = [remote(slot, slot, x_sem.at[chunk, step - 1], ctx, x_peers[step - 1]) for step in (2, 1, 3)]
+
+    written = []
 
     def finish(part):
         for chunk in chunks[part]:
             for copy in along_x[chunk]:
                 copy.wait_recv()
-            rows = rows_of(chunk)
-            for z_idx in range(4):
-                for x_idx in range(4):
-                    first = (x_idx % 2) * HALF
-                    col = head_of(z_idx, x_idx) * HD
-                    grads[part, first + rows.start:first + rows.stop, col:col + HD] = shares[chunk, x_idx, z_idx].astype(F32)
-        copy = pltpu.make_async_copy(grads.at[part], (gk_ref, gv_ref)[part], out_sem.at[part])
-        copy.start()
-        return copy
-
-    lax.fori_loop(0, SLOTS, value_step, 0)
+            written.append(pltpu.make_async_copy(shares.at[chunk], out_ref.at[chunk], out_sem.at[1 + chunk]))
+            written[-1].start()
+
+    lax.fori_loop(0, SLOTS, value_step, 0, unroll=UNROLL)
     by_tokens(VALUES, v_acc, 1.0)
     send_chip(VALUES)
-    lax.fori_loop(0, SLOTS, key_step, 0)
+    lax.fori_loop(0, SLOTS, key_step, 0, unroll=UNROLL)
     send_y(VALUES)
     by_tokens(KEYS, k_acc, SCALE)
     send_chip(KEYS)
@@ -316,25 +303,26 @@
     lax.fori_loop(0, 4, query_step, 0)
     send_y(KEYS)
     lax.fori_loop(4, SLOTS, query_step, 0)
-    send_far(VALUES)
+    send_z(VALUES)
     for half in range(2):
         last = count_0 - 1 if half == 0 else SLOTS - 1
         for unit in range(UNITS):
             layer, head_idx = divmod(unit, HEADS)
             dq_out[layer, half * HALF:(half + 1) * HALF, head_idx * HD:(head_idx + 1) * HD] = (
                 q_acc[last, unit * HALF:(unit + 1) * HALF] * SCALE).astype(BF16)
-    dq_copy = pltpu.make_async_copy(dq_out, dq_ref, out_sem.at[2])
-    dq_copy.start()
-    send_far(KEYS)
-    send_z(VALUES)
+    written.append(pltpu.make_async_copy(dq_out, dq_ref, out_sem.at[0]))
+    written[-1].start()
     send_z(KEYS)
-    pass_on(VALUES)
-    pass_on(KEYS)
-    written = [dq_copy, finish(VALUES), finish(KEYS)]
+    send_x(VALUES)
+    send_x(KEYS)
+    finish(VALUES)
+    finish(KEYS)
     for copy in written:
         copy.wait()
     cross(VALUES, lambda copy: copy.wait_send())
-    for group in (near, over, to_mate, along, across, along_z, along_x):
+    for copy in near[VALUES]:
+        copy.wait_send()
+    for group in (over, to_mate, along, along_z, along_x):
         for copies in group.values():
             for copy in copies:
                 copy.wait_send()
@@ -342,19 +330,38 @@
         copy.wait_send()
 
 
+def place_kernel(off_ref, place_ref):
+    for block in range(BLOCKS):
+        rank = lax.div(off_ref[block], HALF)
+        place_ref[RANK_OF, block] = rank
+        place_ref[BLOCK_AT, rank] = block
+        place_ref[TILE_OF, block] = lax.div(rank, TILE_BLOCKS)
+
+
+def write_kernel(dq_in, share_ref, dq_ref, gk_ref, gv_ref):
+    dq_ref[...] = dq_in[...]
+    for part, ref in enumerate((gk_ref, gv_ref)):
+        for pair in range(2):
+            for z_lo in range(4):
+                col = head_of(z_lo, 2 * pair) * HD
+                ref[:, col:col + HD] = share_ref[part, 0, pair, 0, z_lo].astype(F32)
+
+
 def local(queries, key_heads, value_heads, grad_out, offsets):
-    ranks = jnp.arange(BLOCKS, dtype=jnp.int32)
-    blocks = jnp.sum(jnp.where(offsets[None, :] == ranks[:, None] * HALF, ranks[None, :], 0), axis=1)
-    places = jnp.stack([offsets // HALF, blocks, offsets // TILE])
     dma, vmem = pltpu.SemaphoreType.DMA, pltpu.VMEM
     hbm = pl.BlockSpec(memory_space=pl.ANY)
     smem = pl.BlockSpec(memory_space=pltpu.SMEM)
     grads = jax.ShapeDtypeStruct((TOK, KVH * HD), F32)
-    return pl.pallas_call(
+    dq = jax.ShapeDtypeStruct(queries.shape, BF16)
+    shares = jax.ShapeDtypeStruct((CHUNKS, 4, 4, CHUNK, HD), BF16)
+    places = pl.pallas_call(
+        place_kernel, out_shape=jax.ShapeDtypeStruct((3, BLOCKS), jnp.int32), in_specs=[smem], out_specs=smem,
+        name="places")(offsets)
+    dq_done, shares_done = pl.pallas_call(
         kernel,
-        out_shape=(jax.ShapeDtypeStruct(queries.shape, BF16), grads, grads),
+        out_shape=(dq, shares),
         in_specs=[smem, hbm, hbm, hbm, hbm],
-        out_specs=(hbm, hbm, hbm),
+        out_specs=(hbm, hbm),
         scratch_shapes=[
             vmem((BLOCKS, HALF, HD), BF16), vmem((BLOCKS, HALF, HD), BF16), vmem((TILES, TILE, HD), BF16), vmem((TILES, TILE, HD), BF16),
             vmem((2, ROWS, HD), BF16), vmem((2, ROWS, HD), BF16),
@@ -364,16 +371,27 @@
             vmem((LAYERS, TOK, HEADS * HD), BF16),
             vmem((2, 2, 4, 2, 2, HALF, HD), BF16),
             vmem((CHUNKS, 4, 2, 2, CHUNK, HD), BF16), vmem((CHUNKS, 4, 2, 2, CHUNK, HD), BF16),
-            vmem((CHUNKS, 3, 2, 2, CHUNK, HD), BF16), vmem((CHUNKS, 2, 2, CHUNK, HD), BF16),
-            vmem((CHUNKS, 3, CHUNK, HD), BF16), vmem((CHUNKS, 4, 4, CHUNK, HD), BF16),
-            vmem((2, TOK, KVH * HD), F32),
+            vmem((CHUNKS, 7, 2, CHUNK, HD), BF16), vmem((CHUNKS, 2, CHUNK, HD), BF16),
+            vmem((CHUNKS, 2, 4, CHUNK, HD), BF16), vmem((CHUNKS, 4, 4, CHUNK, HD), BF16),
             dma((2,)), dma((2,)), dma((2, 3)), dma((2, 3, 2)), dma((2, 3, 2)), dma((2, 8, 2)),
-            dma((CHUNKS, 2)), dma((CHUNKS, 3, 2)), dma((CHUNKS, 3, 2)), dma((CHUNKS, 3, 2)), dma((CHUNKS, 4, 3, 2)), dma((3,)),
+            dma((CHUNKS, 2)), dma((CHUNKS, 7, 2)), dma((CHUNKS, 2, 4, 2)), dma((CHUNKS, 3, 2)), dma((1 + CHUNKS,)),
         ],
         compiler_params=pltpu.CompilerParams(collective_id=0, has_side_effects=True, vmem_limit_bytes=58 * 1024 * 1024),
         cost_estimate=pl.CostEstimate(flops=3_400_000_000, bytes_accessed=6_000_000, transcendentals=2_600_000),
         name="attention_backward",
     )(places, queries, grad_out, key_heads.reshape(2, HALF, KVH * HD), value_heads.reshape(2, HALF, KVH * HD))
+    return pl.pallas_call(
+        write_kernel, grid=(2, SPLIT),
+        out_shape=(dq, grads, grads),
+        in_specs=[
+            pl.BlockSpec((LAYERS, CHUNK, HEADS * HD), lambda half, nth: (0, half * SPLIT + nth, 0)),
+            pl.BlockSpec((2, 1, 2, 1, 4, CHUNK, HD), lambda half, nth: (0, nth, 0, half, 0, 0, 0))],
+        out_specs=(
+            pl.BlockSpec((LAYERS, CHUNK, HEADS * HD), lambda half, nth: (0, half * SPLIT + nth, 0)),
+            pl.BlockSpec((CHUNK, KVH * HD), lambda half, nth: (half * SPLIT + nth, 0)),
+            pl.BlockSpec((CHUNK, KVH * HD), lambda half, nth: (half * SPLIT + nth, 0))),
+        name="write_out",
+    )(dq_done, shares_done.reshape(2, SPLIT, 2, 2, 4, CHUNK, HD))
 
 
 def solution(mesh):

time: 68.1 us -> 59.8 us (0.88)
  local copies, waits for them, and re-layouts: 4.78 us -> 0 us
  Pallas kernels: 61.6 us -> 58.7 us
  other arithmetic: 0.78 us -> 0 us
    unnamed x9 -> x0, local copies, waits for them, and re-layouts: 4.78 us -> none
    pallas_call x1 -> x3, Pallas kernels: 61.6 us -> 58.7 us  [the longest x1 53.6 us: local(): pl.pallas_call(kernel, out_shape=(dq, shares), in_specs=[smem, hbm, hbm,...]
where the time goes in v3:
time: 59.8 us; the launch traced here: 59.3 us
  Pallas kernels  58.7 us (98%)
  between operations  0.65 us (1%)
    pallas_call x1, Pallas kernels, local(): pl.pallas_call(kernel, out_shape=(dq, shares), in_specs=[smem, hbm, hbm,...  53.6 us
    pallas_call x1, Pallas kernels, local(): pl.pallas_call(write_kernel, grid=(2, SPLIT), out_shape=(dq, grads, grads...  3.64 us
    pallas_call x1, Pallas kernels, local(): pl.pallas_call(place_kernel, out_shape=jax.ShapeDtypeStruct((3, BLOCKS),...  1.45 us

profile of v3, /device:TPU:8, one launch (start us, length us, event | category | flops | bytes accessed | tf_op | source)
XLA Modules:
  0.0 59.3 jit_solution(4640684356891775735)
XLA Ops:
  0.6 1.5 %places.1.place_ref = s32[3,32]{1,0:T(4,128)} custom-call(s32[32]{0:T(128)} %off_ref.1), custom_call_target="tpu_custom_call" | custom-call | tf_op jit(solution)/shard_map/places/pallas_call | solution.py:357
  2.1 53.6 %attention_backward.1 = (bf16[2,192,512]{2,1,0:T(8,128)(2,1)}, bf16[4,4,4,48,128]{4,3,2,1,0:T(8,128)(2,1)}) custom-call(s32[3,32]{1,0:T(4,128)} %places.1.place_ref, bf16[2,192,512]{2,1,0:T(8,128)(2,1)} %q_ref.1, bf16[2,192,512]{2,1,0:T(8,128)(2,1)} %g_ref.1, bf16[2,96,1024]{2,1,0:T(8,128)(2,1)} %bitcast.4, bf16[2,96,1024]{2,1,0:T(8,128)(2,1)} %bitcast.5), custom_call_target="tpu_custom_call" | custom-call | flops 3400000000 | bytes 6000000 | tf_op jit(solution)/shard_map/attention_backward/pallas_call | solution.py:360
  55.7 3.6 %write_out.1 = (bf16[2,192,512]{2,1,0:T(8,128)(2,1)}, f32[192,1024]{1,0:T(8,128)}, f32[192,1024]{1,0:T(8,128)}) custom-call(bf16[2,192,512]{2,1,0:T(8,128)(2,1)} %get-tuple-element.5.dq_in, bf16[2,2,2,2,4,48,128]{6,5,4,3,2,1,0:T(8,128)(2,1)} %bitcast.3), custom_call_target="tpu_custom_call" | custom-call | tf_op jit(solution)/shard_map/write_out/pallas_call | solution.py:383

commit v4 on v3

--- a/solution.py
+++ b/solution.py
@@ -30,7 +30,6 @@
 F32 = jnp.float32
 UNROLL = 3
 KEYS, VALUES = 0, 1
-RANK_OF, BLOCK_AT, TILE_OF = 0, 1, 2
 
 
 def ctx_of(y, z_hi, core):
@@ -41,8 +40,8 @@
     return z_lo * 2 + x // 2
 
 
-def kernel(place_ref, q_ref, g_ref, k_ref, v_ref, dq_ref, out_ref,
-           all_k, all_v, sorted_k, sorted_v, qs, gs, s_scr, p_scr, d_scr, k_acc, v_acc, q_acc, top_hist, sum_hist, delta_hist, stats, dq_out,
+def kernel(off_ref, q_ref, g_ref, k_ref, v_ref, dq_ref, out_ref,
+           rank_of, block_at, stage, all_k, all_v, sorted_k, sorted_v, qs, gs, s_scr, p_scr, d_scr, k_acc, v_acc, q_acc, top_hist, sum_hist, delta_hist, stats, dq_out,
            parts, chip_in, chip_sum, y_in, y_sum, z_in, shares,
            in_sem, own_sem, cross_sem, near_sem, over_sem, mate_sem, chip_sem, y_sem, z_sem, x_sem, out_sem):
     ctx, kv = lax.axis_index("ctx"), lax.axis_index("kv")
@@ -58,6 +57,30 @@
     nt_dims = (((1,), (1,)), ((), ()))
     tn_dims = (((0,), (0,)), ((), ()))
 
+    barrier = pltpu.get_barrier_semaphore()
+    peers = [(mate, kv)] + [(c, k) for c in y_peers for k in (kv, pair)] + [(ctx, k) for k in x_peers + z_peers]
+    peers += [(far, z_idx * 4 + x) for z_idx in range(4)]
+    for peer in peers:
+        pl.semaphore_signal(barrier, inc=1, device_id=peer, device_id_type=MESH)
+
+    head = head_of(z_lo, x)
+
+    def head_slice(part, head_idx):
+        return (k_ref, v_ref)[part].at[:, :, pl.ds(pl.multiple_of(head_idx * HD, HD), HD)]
+
+    def tokens_of(part, ctx_idx):
+        return (all_k, all_v)[part].at[pl.ds(2 * ctx_idx, 2)]
+
+    cross_to = [jnp.where(at_low, 2 + nth, nth) for nth in range(2)]
+    staged = []
+    for part in (KEYS, VALUES):
+        staged.append([pltpu.make_async_copy(head_slice(part, head), tokens_of(part, ctx), own_sem.at[part, 0])])
+        for nth in range(2):
+            staged[part].append(pltpu.make_async_copy(head_slice(part, head_of(cross_to[nth], x)), stage.at[part, nth],
+                                                      own_sem.at[part, 1 + nth]))
+        for copy in staged[part]:
+            copy.start()
+
     for nth, (ref, dst) in enumerate(((q_ref, qs), (g_ref, gs))):
         for half in range(2):
             for unit in range(UNITS):
@@ -66,11 +89,22 @@
                     ref.at[layer, half * HALF:(half + 1) * HALF, head * HD:(head + 1) * HD],
                     dst.at[half, unit * HALF:(unit + 1) * HALF], in_sem.at[nth]).start()
 
-    barrier = pltpu.get_barrier_semaphore()
-    peers = [(mate, kv)] + [(c, k) for c in y_peers for k in (kv, pair)] + [(ctx, k) for k in x_peers + z_peers]
-    peers += [(far, z_idx * 4 + x) for z_idx in range(4)]
-    for peer in peers:
-        pl.semaphore_signal(barrier, inc=1, device_id=peer, device_id_type=MESH)
+
+    def rank_step(block, _):
+        start = off_ref[block]
+        rank = jnp.int32(0)
+        for other in range(1, BLOCKS):
+            rank += (start >= other * HALF).astype(jnp.int32)
+        rank_of[block] = rank
+        return 0
+
+    def block_step(rank, _):
+        found = jnp.int32(0)
+        for block in range(1, BLOCKS):
+            found += (off_ref[block] == rank * HALF).astype(jnp.int32) * block
+        block_at[rank] = jnp.minimum(found, BLOCKS - 1)
+        return 0
+
     pl.semaphore_wait(barrier, len(peers))
 
     def describe(src, dst, send_sem, recv_sem, ctx_idx, kv_idx):
@@ -82,25 +116,17 @@
         copy.start()
         return copy
 
-    def head_slice(part, head):
-        return (k_ref, v_ref)[part].at[:, :, pl.ds(pl.multiple_of(head * HD, HD), HD)]
-
-    def tokens_of(part, ctx_idx):
-        return (all_k, all_v)[part].at[pl.ds(2 * ctx_idx, 2)]
-
     def cross(part, act):
-        for edge, targets in ((at_low, (2, 3)), (at_high, (1, 0))):
-            @pl.when(edge)
-            def _():
-                for nth, target in enumerate(targets):
-                    act(describe(head_slice(part, head_of(target, x)), tokens_of(part, ctx),
-                                 cross_sem.at[part, 1 + nth], cross_sem.at[part, 0], far, target * 4 + x))
-
-    head = head_of(z_lo, x)
+        @pl.when(jnp.logical_or(at_low, at_high))
+        def _():
+            for nth in range(2):
+                act(describe(stage.at[part, nth], tokens_of(part, ctx), cross_sem.at[part, 1 + nth], cross_sem.at[part, 0],
+                             far, cross_to[nth] * 4 + x))
+
     near, over, to_mate = {}, {}, {}
 
     def send_near(part):
-        near[part] = [remote(head_slice(part, head), tokens_of(part, ctx), near_sem.at[part, step - 1], y_peers[step - 1], kv)
+        near[part] = [remote(tokens_of(part, ctx), tokens_of(part, ctx), near_sem.at[part, step - 1], y_peers[step - 1], kv)
                       for step in (1, 2, 3)]
 
     def send_over(part):
@@ -113,20 +139,19 @@
         to_mate.setdefault(part, []).append(
             remote(tokens_of(part, idx), tokens_of(part, idx), mate_sem.at[part, len(to_mate.get(part, []))], mate, kv))
 
-    own = [pltpu.make_async_copy(head_slice(part, head), tokens_of(part, ctx), own_sem.at[part]) for part in (KEYS, VALUES)]
+    for part in (KEYS, VALUES):
+        for copy in staged[part]:
+            copy.wait()
     cross(KEYS, lambda copy: copy.start())
     send_near(KEYS)
-    for copy in own:
-        copy.start()
     cross(KEYS, lambda copy: copy.wait_send())
     cross(VALUES, lambda copy: copy.start())
-    own[KEYS].wait()
     send_mate(KEYS, 0, z_hi)
     for copy in near[KEYS]:
         copy.wait_send()
     send_near(VALUES)
-    own[VALUES].wait()
     send_mate(VALUES, 0, z_hi)
+    lax.fori_loop(0, BLOCKS, block_step, 0)
     send_over(KEYS)
     send_mate(KEYS, 0, 1 - z_hi)
     for step in (1, 3, 2):
@@ -134,6 +159,7 @@
         send_mate(KEYS, step, z_hi)
     send_over(VALUES)
     send_mate(VALUES, 0, 1 - z_hi)
+    lax.fori_loop(0, BLOCKS, rank_step, 0)
     for step in (1, 3, 2):
         over[KEYS][step - 1].wait_recv()
         send_mate(KEYS, step, 1 - z_hi)
@@ -146,14 +172,14 @@
     def sort(part):
         for rank in range(BLOCKS):
             first = rank % TILE_BLOCKS * HALF
-            (sorted_k, sorted_v)[part][rank // TILE_BLOCKS, first:first + HALF] = (all_k, all_v)[part][place_ref[BLOCK_AT, rank]]
+            (sorted_k, sorted_v)[part][rank // TILE_BLOCKS, first:first + HALF] = (all_k, all_v)[part][block_at[rank]]
 
     sort(KEYS)
     pltpu.make_async_copy(qs, qs, in_sem.at[0]).wait()
     pltpu.make_async_copy(gs, gs, in_sem.at[1]).wait()
 
-    start_0, start_1 = place_ref[RANK_OF, 2 * ctx] * HALF, place_ref[RANK_OF, 2 * ctx + 1] * HALF
-    count_0 = place_ref[TILE_OF, 2 * ctx] + 1
+    start_0, start_1 = off_ref[2 * ctx], off_ref[2 * ctx + 1]
+    count_0 = sum(((start_0 >= tile * TILE).astype(jnp.int32) for tile in range(1, TILES)), jnp.int32(1))
     count_1 = SLOTS - count_0
 
     def slot_of(slot):
@@ -228,7 +254,7 @@
 
     def by_tokens(part, acc, scale):
         for block in range(BLOCKS):
-            rank = place_ref[RANK_OF, block]
+            rank = rank_of[block]
             in_0 = (rank < count_0 * TILE_BLOCKS).astype(jnp.int32)
             in_1 = (rank < count_1 * TILE_BLOCKS).astype(jnp.int32)
             both = (acc[rank * in_0] * (in_0.astype(F32) * scale)
@@ -302,8 +328,9 @@
     q_acc[0] = jnp.zeros((ROWS, HD), F32)
     lax.fori_loop(0, 4, query_step, 0)
     send_y(KEYS)
-    lax.fori_loop(4, SLOTS, query_step, 0)
+    lax.fori_loop(4, 7, query_step, 0)
     send_z(VALUES)
+    lax.fori_loop(7, SLOTS, query_step, 0)
     for half in range(2):
         last = count_0 - 1 if half == 0 else SLOTS - 1
         for unit in range(UNITS):
@@ -330,21 +357,32 @@
         copy.wait_send()
 
 
-def place_kernel(off_ref, place_ref):
-    for block in range(BLOCKS):
-        rank = lax.div(off_ref[block], HALF)
-        place_ref[RANK_OF, block] = rank
-        place_ref[BLOCK_AT, rank] = block
-        place_ref[TILE_OF, block] = lax.div(rank, TILE_BLOCKS)
-
-
-def write_kernel(dq_in, share_ref, dq_ref, gk_ref, gv_ref):
-    dq_ref[...] = dq_in[...]
-    for part, ref in enumerate((gk_ref, gv_ref)):
-        for pair in range(2):
-            for z_lo in range(4):
-                col = head_of(z_lo, 2 * pair) * HD
-                ref[:, col:col + HD] = share_ref[part, 0, pair, 0, z_lo].astype(F32)
+def write_kernel(dq_in, share_in, dq_ref, gk_ref, gv_ref, dq_buf, shares, grads, in_sem, out_sem):
+    dq_load = pltpu.make_async_copy(dq_in, dq_buf, in_sem.at[CHUNKS])
+    loads = [pltpu.make_async_copy(share_in.at[chunk], shares.at[chunk], in_sem.at[chunk]) for chunk in range(CHUNKS)]
+    for copy in loads + [dq_load]:
+        copy.start()
+    stores = []
+
+    def store(src, dst):
+        stores.append(pltpu.make_async_copy(src, dst, out_sem.at[len(stores)]))
+        stores[-1].start()
+
+    for part, ref in ((KEYS, gk_ref), (VALUES, gv_ref)):
+        for nth in range(SPLIT):
+            chunk = part * SPLIT + nth
+            loads[chunk].wait()
+            for half in range(2):
+                rows = slice(half * HALF + nth * CHUNK, half * HALF + (nth + 1) * CHUNK)
+                for x in (half, half + 2):
+                    for z_lo in range(4):
+                        col = head_of(z_lo, x) * HD
+                        grads[part, rows, col:col + HD] = shares[chunk, x, z_lo].astype(F32)
+                store(grads.at[part, rows], ref.at[rows])
+    dq_load.wait()
+    store(dq_buf, dq_ref)
+    for copy in stores:
+        copy.wait()
 
 
 def local(queries, key_heads, value_heads, grad_out, offsets):
@@ -354,15 +392,13 @@
     grads = jax.ShapeDtypeStruct((TOK, KVH * HD), F32)
     dq = jax.ShapeDtypeStruct(queries.shape, BF16)
     shares = jax.ShapeDtypeStruct((CHUNKS, 4, 4, CHUNK, HD), BF16)
-    places = pl.pallas_call(
-        place_kernel, out_shape=jax.ShapeDtypeStruct((3, BLOCKS), jnp.int32), in_specs=[smem], out_specs=smem,
-        name="places")(offsets)
     dq_done, shares_done = pl.pallas_call(
         kernel,
         out_shape=(dq, shares),
         in_specs=[smem, hbm, hbm, hbm, hbm],
         out_specs=(hbm, hbm),
         scratch_shapes=[
+            pltpu.SMEM((BLOCKS,), jnp.int32), pltpu.SMEM((BLOCKS,), jnp.int32), vmem((2, 2, 2, HALF, HD), BF16),
             vmem((BLOCKS, HALF, HD), BF16), vmem((BLOCKS, HALF, HD), BF16), vmem((TILES, TILE, HD), BF16), vmem((TILES, TILE, HD), BF16),
             vmem((2, ROWS, HD), BF16), vmem((2, ROWS, HD), BF16),
             vmem((SLOTS * TILE, ROWS), F32), vmem((SLOTS * TILE, ROWS), F32), vmem((SLOTS * TILE, ROWS), BF16),
@@ -373,25 +409,23 @@
             vmem((CHUNKS, 4, 2, 2, CHUNK, HD), BF16), vmem((CHUNKS, 4, 2, 2, CHUNK, HD), BF16),
             vmem((CHUNKS, 7, 2, CHUNK, HD), BF16), vmem((CHUNKS, 2, CHUNK, HD), BF16),
             vmem((CHUNKS, 2, 4, CHUNK, HD), BF16), vmem((CHUNKS, 4, 4, CHUNK, HD), BF16),
-            dma((2,)), dma((2,)), dma((2, 3)), dma((2, 3, 2)), dma((2, 3, 2)), dma((2, 8, 2)),
+            dma((2,)), dma((2, 3)), dma((2, 3)), dma((2, 3, 2)), dma((2, 3, 2)), dma((2, 8, 2)),
             dma((CHUNKS, 2)), dma((CHUNKS, 7, 2)), dma((CHUNKS, 2, 4, 2)), dma((CHUNKS, 3, 2)), dma((1 + CHUNKS,)),
         ],
         compiler_params=pltpu.CompilerParams(collective_id=0, has_side_effects=True, vmem_limit_bytes=58 * 1024 * 1024),
         cost_estimate=pl.CostEstimate(flops=3_400_000_000, bytes_accessed=6_000_000, transcendentals=2_600_000),
         name="attention_backward",
-    )(places, queries, grad_out, key_heads.reshape(2, HALF, KVH * HD), value_heads.reshape(2, HALF, KVH * HD))
+    )(offsets, queries, grad_out, key_heads.reshape(2, HALF, KVH * HD), value_heads.reshape(2, HALF, KVH * HD))
     return pl.pallas_call(
-        write_kernel, grid=(2, SPLIT),
+        write_kernel,
         out_shape=(dq, grads, grads),
-        in_specs=[
-            pl.BlockSpec((LAYERS, CHUNK, HEADS * HD), lambda half, nth: (0, half * SPLIT + nth, 0)),
-            pl.BlockSpec((2, 1, 2, 1, 4, CHUNK, HD), lambda half, nth: (0, nth, 0, half, 0, 0, 0))],
-        out_specs=(
-            pl.BlockSpec((LAYERS, CHUNK, HEADS * HD), lambda half, nth: (0, half * SPLIT + nth, 0)),
-            pl.BlockSpec((CHUNK, KVH * HD), lambda half, nth: (half * SPLIT + nth, 0)),
-            pl.BlockSpec((CHUNK, KVH * HD), lambda half, nth: (half * SPLIT + nth, 0))),
+        in_specs=[hbm, hbm],
+        out_specs=(hbm, hbm, hbm),
+        scratch_shapes=[vmem(queries.shape, BF16), vmem(shares.shape, BF16), vmem((2, TOK, KVH * HD), F32),
+                        dma((CHUNKS + 1,)), dma((2 * CHUNKS + 1,))],
+        compiler_params=pltpu.CompilerParams(vmem_limit_bytes=58 * 1024 * 1024),
         name="write_out",
-    )(dq_done, shares_done.reshape(2, SPLIT, 2, 2, 4, CHUNK, HD))
+    )(dq_done, shares_done)
 
 
 def solution(mesh):

time: 59.8 us -> 56.5 us (0.945)
  Pallas kernels: 58.7 us -> 55.7 us
    pallas_call x2 -> x1, Pallas kernels: 5.09 us -> 2.33 us  [local(): pl.pallas_call(write_kernel, out_shape=(dq, grads, grads), in_specs=[hbm,...]
where the time goes in v4:
time: 56.5 us; the launch traced here: 56.3 us
  Pallas kernels  55.7 us (99%)
  between operations  0.64 us (1%)
    pallas_call x1, Pallas kernels, local(): pl.pallas_call(kernel, out_shape=(dq, shares), in_specs=[smem, hbm, hbm,...  53.4 us
    pallas_call x1, Pallas kernels, local(): pl.pallas_call(write_kernel, out_shape=(dq, grads, grads), in_specs=[hbm,...  2.33 us

profile of v4, /device:TPU:8, one launch (start us, length us, event | category | flops | bytes accessed | tf_op | source)
XLA Modules:
  0.0 56.3 jit_solution(5736398967013885074)
XLA Ops:
  0.6 53.4 %attention_backward.1 = (bf16[2,192,512]{2,1,0:T(8,128)(2,1)}, bf16[4,4,4,48,128]{4,3,2,1,0:T(8,128)(2,1)}) custom-call(s32[32]{0:T(128)} %off_ref.1, bf16[2,192,512]{2,1,0:T(8,128)(2,1)} %q_ref.1, bf16[2,192,512]{2,1,0:T(8,128)(2,1)} %g_ref.1, bf16[2,96,1024]{2,1,0:T(8,128)(2,1)} %bitcast.2, bf16[2,96,1024]{2,1,0:T(8,128)(2,1)} %bitcast.3), custom_call_target="tpu_custom_call" | custom-call | flops 3400000000 | bytes 6000000 | tf_op jit(solution)/shard_map/attention_backward/pallas_call | solution.py:395
  54.0 2.3 %write_out.1 = (bf16[2,192,512]{2,1,0:T(8,128)(2,1)}, f32[192,1024]{1,0:T(8,128)}, f32[192,1024]{1,0:T(8,128)}) custom-call(bf16[2,192,512]{2,1,0:T(8,128)(2,1)} %get-tuple-element.5.dq_in, bf16[4,4,4,48,128]{4,3,2,1,0:T(8,128)(2,1)} %get-tuple-element.6.share_in), custom_call_target="tpu_custom_call" | custom-call | tf_op jit(solution)/shard_map/write_out/pallas_call | solution.py:419

commit v5 on v4

--- a/solution.py
+++ b/solution.py
@@ -58,8 +58,7 @@
     tn_dims = (((0,), (0,)), ((), ()))
 
     barrier = pltpu.get_barrier_semaphore()
-    peers = [(mate, kv)] + [(c, k) for c in y_peers for k in (kv, pair)] + [(ctx, k) for k in x_peers + z_peers]
-    peers += [(far, z_idx * 4 + x) for z_idx in range(4)]
+    peers = [(far, z_idx * 4 + x) for z_idx in range(4)] + [(mate, kv)] + [(c, k) for c in y_peers for k in (kv, pair)] + [(ctx, k) for k in x_peers + z_peers]
     for peer in peers:
         pl.semaphore_signal(barrier, inc=1, device_id=peer, device_id_type=MESH)
 
@@ -69,7 +68,7 @@
         return (k_ref, v_ref)[part].at[:, :, pl.ds(pl.multiple_of(head_idx * HD, HD), HD)]
 
     def tokens_of(part, ctx_idx):
-        return (all_k, all_v)[part].at[pl.ds(2 * ctx_idx, 2)]
+        return (all_k, all_v)[part].at[ctx_idx // 4, ctx_idx // 2 % 2, ctx_idx % 2]
 
     cross_to = [jnp.where(at_low, 2 + nth, nth) for nth in range(2)]
     staged = []
@@ -81,6 +80,58 @@
         for copy in staged[part]:
             copy.start()
 
+    def rank_step(block, _):
+        start = off_ref[block]
+        rank = jnp.int32(0)
+        for other in range(1, BLOCKS):
+            rank += (start >= other * HALF).astype(jnp.int32)
+        rank_of[block] = rank
+        return 0
+
+    def block_step(rank, _):
+        found = jnp.int32(0)
+        for block in range(1, BLOCKS):
+            found += (off_ref[block] == rank * HALF).astype(jnp.int32) * block
+        block_at[rank] = jnp.minimum(found, BLOCKS - 1)
+        return 0
+
+    pl.semaphore_wait(barrier, len(peers))
+
+    def describe(src, dst, send_sem, recv_sem, ctx_idx, kv_idx):
+        return pltpu.make_async_remote_copy(src_ref=src, dst_ref=dst, send_sem=send_sem, recv_sem=recv_sem,
+                                            device_id=(ctx_idx, kv_idx), device_id_type=MESH)
+
+    def remote(src, dst, sems, ctx_idx, kv_idx):
+        copy = describe(src, dst, sems.at[0], sems.at[1], ctx_idx, kv_idx)
+        copy.start()
+        return copy
+
+    def cross(part, act):
+        @pl.when(jnp.logical_or(at_low, at_high))
+        def _():
+            for nth in range(2):
+                act(describe(stage.at[part, nth], tokens_of(part, ctx), cross_sem.at[part, 1 + nth], cross_sem.at[part, 0],
+                             far, cross_to[nth] * 4 + x))
+
+    near, over, to_mate = {}, {}, {}
+
+    def send_near(part):
+        near[part] = [remote(tokens_of(part, ctx), tokens_of(part, ctx), near_sem.at[part, step - 1], y_peers[step - 1], kv)
+                      for step in (1, 2, 3)]
+
+    def send_over(part):
+        pltpu.make_async_copy(tokens_of(part, far), tokens_of(part, far), cross_sem.at[part, 0]).wait()
+        over[part] = [remote(tokens_of(part, far), tokens_of(part, far), over_sem.at[part, step - 1], y_peers[step - 1], kv)
+                      for step in (1, 2, 3)]
+
+    def send_mate(part, half):
+        src = (all_k, all_v)[part].at[:, half, core]
+        to_mate.setdefault(part, []).append(remote(src, src, mate_sem.at[part, len(to_mate.get(part, []))], mate, kv))
+
+    for copy in staged[KEYS]:
+        copy.wait()
+    cross(KEYS, lambda copy: copy.start())
+    send_near(KEYS)
     for nth, (ref, dst) in enumerate(((q_ref, qs), (g_ref, gs))):
         for half in range(2):
             for unit in range(UNITS):
@@ -88,91 +139,35 @@
                 pltpu.make_async_copy(
                     ref.at[layer, half * HALF:(half + 1) * HALF, head * HD:(head + 1) * HD],
                     dst.at[half, unit * HALF:(unit + 1) * HALF], in_sem.at[nth]).start()
-
-
-    def rank_step(block, _):
-        start = off_ref[block]
-        rank = jnp.int32(0)
-        for other in range(1, BLOCKS):
-            rank += (start >= other * HALF).astype(jnp.int32)
-        rank_of[block] = rank
-        return 0
-
-    def block_step(rank, _):
-        found = jnp.int32(0)
-        for block in range(1, BLOCKS):
-            found += (off_ref[block] == rank * HALF).astype(jnp.int32) * block
-        block_at[rank] = jnp.minimum(found, BLOCKS - 1)
-        return 0
-
-    pl.semaphore_wait(barrier, len(peers))
-
-    def describe(src, dst, send_sem, recv_sem, ctx_idx, kv_idx):
-        return pltpu.make_async_remote_copy(src_ref=src, dst_ref=dst, send_sem=send_sem, recv_sem=recv_sem,
-                                            device_id=(ctx_idx, kv_idx), device_id_type=MESH)
-
-    def remote(src, dst, sems, ctx_idx, kv_idx):
-        copy = describe(src, dst, sems.at[0], sems.at[1], ctx_idx, kv_idx)
-        copy.start()
-        return copy
-
-    def cross(part, act):
-        @pl.when(jnp.logical_or(at_low, at_high))
-        def _():
-            for nth in range(2):
-                act(describe(stage.at[part, nth], tokens_of(part, ctx), cross_sem.at[part, 1 + nth], cross_sem.at[part, 0],
-                             far, cross_to[nth] * 4 + x))
-
-    near, over, to_mate = {}, {}, {}
-
-    def send_near(part):
-        near[part] = [remote(tokens_of(part, ctx), tokens_of(part, ctx), near_sem.at[part, step - 1], y_peers[step - 1], kv)
-                      for step in (1, 2, 3)]
-
-    def send_over(part):
-        pltpu.make_async_copy(tokens_of(part, far), tokens_of(part, far), cross_sem.at[part, 0]).wait()
-        over[part] = [remote(tokens_of(part, far), tokens_of(part, far), over_sem.at[part, step - 1], y_peers[step - 1], kv)
-                      for step in (1, 2, 3)]
-
-    def send_mate(part, step, half):
-        idx = ctx_of((y - step + 4) % 4, half, core)
-        to_mate.setdefault(part, []).append(
-            remote(tokens_of(part, idx), tokens_of(part, idx), mate_sem.at[part, len(to_mate.get(part, []))], mate, kv))
-
-    for part in (KEYS, VALUES):
-        for copy in staged[part]:
-            copy.wait()
-    cross(KEYS, lambda copy: copy.start())
-    send_near(KEYS)
+    for copy in staged[VALUES]:
+        copy.wait()
     cross(KEYS, lambda copy: copy.wait_send())
     cross(VALUES, lambda copy: copy.start())
-    send_mate(KEYS, 0, z_hi)
     for copy in near[KEYS]:
         copy.wait_send()
     send_near(VALUES)
-    send_mate(VALUES, 0, z_hi)
     lax.fori_loop(0, BLOCKS, block_step, 0)
     send_over(KEYS)
-    send_mate(KEYS, 0, 1 - z_hi)
-    for step in (1, 3, 2):
-        near[KEYS][step - 1].wait_recv()
-        send_mate(KEYS, step, z_hi)
+    for copy in near[KEYS]:
+        copy.wait_recv()
+    send_mate(KEYS, z_hi)
     send_over(VALUES)
-    send_mate(VALUES, 0, 1 - z_hi)
     lax.fori_loop(0, BLOCKS, rank_step, 0)
-    for step in (1, 3, 2):
-        over[KEYS][step - 1].wait_recv()
-        send_mate(KEYS, step, 1 - z_hi)
-    for step in (1, 3, 2):
-        near[VALUES][step - 1].wait_recv()
-        send_mate(VALUES, step, z_hi)
+    for copy in over[KEYS]:
+        copy.wait_recv()
+    send_mate(KEYS, 1 - z_hi)
+    for copy in near[VALUES]:
+        copy.wait_recv()
+    send_mate(VALUES, z_hi)
     for copy in to_mate[KEYS]:
         copy.wait_recv()
+
+    by_block = [ref.reshape(BLOCKS, HALF, HD) for ref in (all_k, all_v)]
 
     def sort(part):
         for rank in range(BLOCKS):
             first = rank % TILE_BLOCKS * HALF
-            (sorted_k, sorted_v)[part][rank // TILE_BLOCKS, first:first + HALF] = (all_k, all_v)[part][block_at[rank]]
+            (sorted_k, sorted_v)[part][rank // TILE_BLOCKS, first:first + HALF] = by_block[part][block_at[rank]]
 
     sort(KEYS)
     pltpu.make_async_copy(qs, qs, in_sem.at[0]).wait()
@@ -205,9 +200,9 @@
         return top
 
     top = lax.fori_loop(0, SLOTS - UNROLL, score_step, jnp.full((8, ROWS), -1e30, F32), unroll=UNROLL)
-    for step in (1, 3, 2):
-        over[VALUES][step - 1].wait_recv()
-        send_mate(VALUES, step, 1 - z_hi)
+    for copy in over[VALUES]:
+        copy.wait_recv()
+    send_mate(VALUES, 1 - z_hi)
     lax.fori_loop(SLOTS - UNROLL, SLOTS, score_step, top, unroll=UNROLL)
     for half, last in enumerate((count_0 - 1, SLOTS - 1)):
         stats[half, 0] = jnp.broadcast_to(jnp.max(top_hist[last], axis=0, keepdims=True), (8, ROWS))
@@ -262,7 +257,7 @@
             parts[part, block // 2 % 2, block // 8, block % 2, block // 4 % 2] = both.astype(BF16)
 
     chunks = {KEYS: range(SPLIT), VALUES: range(SPLIT, CHUNKS)}
-    chip, along, along_z, along_x = {}, {}, {}, {}
+    chip, along, along_z, along_x, written = {}, {}, {}, {}, []
 
     def rows_of(chunk):
         return slice(chunk % SPLIT * CHUNK, (chunk % SPLIT + 1) * CHUNK)
@@ -305,20 +300,13 @@
         for chunk in chunks[part]:
             for copy in along_z[chunk]:
                 copy.wait_recv()
-            shares[chunk, x] = (z_in[chunk, 0].astype(F32) + z_in[chunk, 1].astype(F32)).astype(BF16)
-            slot = shares.at[chunk, x]
-            along_x[chunk] = [remote(slot, slot, x_sem.at[chunk, step - 1], ctx, x_peers[step - 1]) for step in (2, 1, 3)]
-
-    written = []
-
-    def finish(part):
-        for chunk in chunks[part]:
-            for copy in along_x[chunk]:
-                copy.wait_recv()
-            written.append(pltpu.make_async_copy(shares.at[chunk], out_ref.at[chunk], out_sem.at[1 + chunk]))
+            shares[chunk] = (z_in[chunk, 0].astype(F32) + z_in[chunk, 1].astype(F32)).astype(BF16)
+            src, dst = shares.at[chunk], out_ref.at[chunk, x]
+            along_x[chunk] = [remote(src, dst, x_sem.at[chunk, step - 1], ctx, x_peers[step - 1]) for step in (2, 1, 3)]
+            written.append(pltpu.make_async_copy(src, dst, out_sem.at[1 + chunk]))
             written[-1].start()
 
-    lax.fori_loop(0, SLOTS, value_step, 0, unroll=UNROLL)
+    lax.fori_loop(0, SLOTS, value_step, 0, unroll=SLOTS)
     by_tokens(VALUES, v_acc, 1.0)
     send_chip(VALUES)
     lax.fori_loop(0, SLOTS, key_step, 0, unroll=UNROLL)
@@ -342,19 +330,19 @@
     send_z(KEYS)
     send_x(VALUES)
     send_x(KEYS)
-    finish(VALUES)
-    finish(KEYS)
-    for copy in written:
-        copy.wait()
     cross(VALUES, lambda copy: copy.wait_send())
-    for copy in near[VALUES]:
+    for copy in near[VALUES] + list(chip.values()):
         copy.wait_send()
-    for group in (over, to_mate, along, along_z, along_x):
+    for group in (over, to_mate, along, along_z):
         for copies in group.values():
             for copy in copies:
                 copy.wait_send()
-    for copy in chip.values():
-        copy.wait_send()
+    for copy in written:
+        copy.wait()
+    for part in (VALUES, KEYS):
+        for chunk in chunks[part]:
+            for copy in along_x[chunk]:
+                copy.wait()
 
 
 def write_kernel(dq_in, share_in, dq_ref, gk_ref, gv_ref, dq_buf, shares, grads, in_sem, out_sem):
@@ -399,7 +387,7 @@
         out_specs=(hbm, hbm),
         scratch_shapes=[
             pltpu.SMEM((BLOCKS,), jnp.int32), pltpu.SMEM((BLOCKS,), jnp.int32), vmem((2, 2, 2, HALF, HD), BF16),
-            vmem((BLOCKS, HALF, HD), BF16), vmem((BLOCKS, HALF, HD), BF16), vmem((TILES, TILE, HD), BF16), vmem((TILES, TILE, HD), BF16),
+            vmem((4, 2, 2, 2, HALF, HD), BF16), vmem((4, 2, 2, 2, HALF, HD), BF16), vmem((TILES, TILE, HD), BF16), vmem((TILES, TILE, HD), BF16),
             vmem((2, ROWS, HD), BF16), vmem((2, ROWS, HD), BF16),
             vmem((SLOTS * TILE, ROWS), F32), vmem((SLOTS * TILE, ROWS), F32), vmem((SLOTS * TILE, ROWS), BF16),
             vmem((SLOTS * TILE_BLOCKS, HALF, HD), F32), vmem((SLOTS * TILE_BLOCKS, HALF, HD), F32), vmem((SLOTS, ROWS, HD), F32),
@@ -408,8 +396,8 @@
             vmem((2, 2, 4, 2, 2, HALF, HD), BF16),
             vmem((CHUNKS, 4, 2, 2, CHUNK, HD), BF16), vmem((CHUNKS, 4, 2, 2, CHUNK, HD), BF16),
             vmem((CHUNKS, 7, 2, CHUNK, HD), BF16), vmem((CHUNKS, 2, CHUNK, HD), BF16),
-            vmem((CHUNKS, 2, 4, CHUNK, HD), BF16), vmem((CHUNKS, 4, 4, CHUNK, HD), BF16),
-            dma((2,)), dma((2, 3)), dma((2, 3)), dma((2, 3, 2)), dma((2, 3, 2)), dma((2, 8, 2)),
+            vmem((CHUNKS, 2, 4, CHUNK, HD), BF16), vmem((CHUNKS, 4, CHUNK, HD), BF16),
+            dma((2,)), dma((2, 3)), dma((2, 3)), dma((2, 3, 2)), dma((2, 3, 2)), dma((2, 2, 2)),
             dma((CHUNKS, 2)), dma((CHUNKS, 7, 2)), dma((CHUNKS, 2, 4, 2)), dma((CHUNKS, 3, 2)), dma((1 + CHUNKS,)),
         ],
         compiler_params=pltpu.CompilerParams(collective_id=0, has_side_effects=True, vmem_limit_bytes=58 * 1024 * 1024),

time: 56.5 us -> 55.2 us (0.977)
  Pallas kernels: 55.7 us -> 54.4 us
    pallas_call x1, Pallas kernels: 53.4 us -> 52.1 us  [local(): pl.pallas_call(kernel, out_shape=(dq, shares), in_specs=[smem, hbm, hbm,...]
where the time goes in v5:
time: 55.2 us; the launch traced here: 55 us
  Pallas kernels  54.4 us (99%)
  between operations  0.64 us (1%)
    pallas_call x1, Pallas kernels, local(): pl.pallas_call(kernel, out_shape=(dq, shares), in_specs=[smem, hbm, hbm,...  52.1 us
    pallas_call x1, Pallas kernels, local(): pl.pallas_call(write_kernel, out_shape=(dq, grads, grads), in_specs=[hbm,...  2.33 us

profile of v5, /device:TPU:8, one launch (start us, length us, event | category | flops | bytes accessed | tf_op | source)
XLA Modules:
  0.0 55.0 jit_solution(14588156080331704060)
XLA Ops:
  0.6 52.1 %attention_backward.1 = (bf16[2,192,512]{2,1,0:T(8,128)(2,1)}, bf16[4,4,4,48,128]{4,3,2,1,0:T(8,128)(2,1)}) custom-call(s32[32]{0:T(128)} %off_ref.1, bf16[2,192,512]{2,1,0:T(8,128)(2,1)} %q_ref.1, bf16[2,192,512]{2,1,0:T(8,128)(2,1)} %g_ref.1, bf16[2,96,1024]{2,1,0:T(8,128)(2,1)} %bitcast.2, bf16[2,96,1024]{2,1,0:T(8,128)(2,1)} %bitcast.3), custom_call_target="tpu_custom_call" | custom-call | flops 3400000000 | bytes 6000000 | tf_op jit(solution)/shard_map/attention_backward/pallas_call | solution.py:383
  52.7 2.3 %write_out.1 = (bf16[2,192,512]{2,1,0:T(8,128)(2,1)}, f32[192,1024]{1,0:T(8,128)}, f32[192,1024]{1,0:T(8,128)}) custom-call(bf16[2,192,512]{2,1,0:T(8,128)(2,1)} %get-tuple-element.5.dq_in, bf16[4,4,4,48,128]{4,3,2,1,0:T(8,128)(2,1)} %get-tuple-element.6.share_in), custom_call_target="tpu_custom_call" | custom-call | tf_op jit(solution)/shard_map/write_out/pallas_call | solution.py:407

commit v6 on v5

--- a/solution.py
+++ b/solution.py
@@ -233,12 +233,14 @@
         half, tile, keys, rows = slot_of(slot)
         prob = s_scr[rows] * stats[half, 1][:1]
         v_acc[pl.ds(slot * TILE_BLOCKS, TILE_BLOCKS)] = jnp.dot(prob.astype(BF16), gs[half], preferred_element_type=F32).reshape(TILE_BLOCKS, HALF, HD)
-        d_scr[rows] = (prob * (p_scr[rows] - stats[half, 2][:1])).astype(BF16)
         return 0
 
     def key_step(slot, _):
         half, tile, keys, rows = slot_of(slot)
-        k_acc[pl.ds(slot * TILE_BLOCKS, TILE_BLOCKS)] = jnp.dot(d_scr[rows], qs[half], preferred_element_type=F32).reshape(TILE_BLOCKS, HALF, HD)
+        prob = s_scr[rows] * stats[half, 1][:1]
+        grad_scores = (prob * (p_scr[rows] - stats[half, 2][:1])).astype(BF16)
+        d_scr[rows] = grad_scores
+        k_acc[pl.ds(slot * TILE_BLOCKS, TILE_BLOCKS)] = jnp.dot(grad_scores, qs[half], preferred_element_type=F32).reshape(TILE_BLOCKS, HALF, HD)
         return 0
 
     def query_step(slot, _):
@@ -247,14 +249,14 @@
         q_acc[slot] = term + q_acc[jnp.maximum(slot - 1, 0)] * carried(slot)
         return 0
 
-    def by_tokens(part, acc, scale):
+    def by_tokens(part, acc, scale, span):
         for block in range(BLOCKS):
             rank = rank_of[block]
             in_0 = (rank < count_0 * TILE_BLOCKS).astype(jnp.int32)
             in_1 = (rank < count_1 * TILE_BLOCKS).astype(jnp.int32)
-            both = (acc[rank * in_0] * (in_0.astype(F32) * scale)
-                    + acc[(count_0 * TILE_BLOCKS + rank) * in_1] * (in_1.astype(F32) * scale))
-            parts[part, block // 2 % 2, block // 8, block % 2, block // 4 % 2] = both.astype(BF16)
+            both = (acc[rank * in_0, span] * (in_0.astype(F32) * scale)
+                    + acc[(count_0 * TILE_BLOCKS + rank) * in_1, span] * (in_1.astype(F32) * scale))
+            parts[part, block // 2 % 2, block // 8, block % 2, block // 4 % 2, span] = both.astype(BF16)
 
     chunks = {KEYS: range(SPLIT), VALUES: range(SPLIT, CHUNKS)}
     chip, along, along_z, along_x, written = {}, {}, {}, {}, []
@@ -262,8 +264,9 @@
     def rows_of(chunk):
         return slice(chunk % SPLIT * CHUNK, (chunk % SPLIT + 1) * CHUNK)
 
-    def send_chip(part):
+    def send_chip(part, acc, scale):
         for chunk in chunks[part]:
+            by_tokens(part, acc, scale, rows_of(chunk))
             chip[chunk] = remote(parts.at[part, 1 - core, :, :, :, rows_of(chunk)], chip_in.at[chunk], chip_sem.at[chunk], mate, kv)
 
     def send_y(part):
@@ -275,7 +278,7 @@
                 both = parts[part, core, to_y, :, :, rows_of(chunk)].astype(F32) + chip_in[chunk, to_y].astype(F32)
                 chip_sum[chunk, step] = both.astype(BF16)
                 to_ctx = y_peers[step - 1] if step else ctx
-                for other in ((1, 0) if step else (1,)):
+                for other in ((0, 1) if step else (1,)):
                     nth = 2 * step + other - 1
                     along[chunk].append(remote(chip_sum.at[chunk, step, 1 - odd if other else odd], y_in.at[chunk, nth],
                                                y_sem.at[chunk, nth], to_ctx, pair if other else kv))
@@ -307,16 +310,14 @@
             written[-1].start()
 
     lax.fori_loop(0, SLOTS, value_step, 0, unroll=SLOTS)
-    by_tokens(VALUES, v_acc, 1.0)
-    send_chip(VALUES)
+    send_chip(VALUES, v_acc, 1.0)
     lax.fori_loop(0, SLOTS, key_step, 0, unroll=UNROLL)
     send_y(VALUES)
-    by_tokens(KEYS, k_acc, SCALE)
-    send_chip(KEYS)
+    send_chip(KEYS, k_acc, SCALE)
     q_acc[0] = jnp.zeros((ROWS, HD), F32)
-    lax.fori_loop(0, 4, query_step, 0)
+    lax.fori_loop(0, 3, query_step, 0)
     send_y(KEYS)
-    lax.fori_loop(4, 7, query_step, 0)
+    lax.fori_loop(3, 7, query_step, 0)
     send_z(VALUES)
     lax.fori_loop(7, SLOTS, query_step, 0)
     for half in range(2):

time: 55.2 us -> 55.2 us (level)
  no operation moved by 1% of the time
where the time goes in v6:
time: 55.2 us; the launch traced here: 55 us
  Pallas kernels  54.4 us (99%)
  between operations  0.64 us (1%)
    pallas_call x1, Pallas kernels, local(): pl.pallas_call(kernel, out_shape=(dq, shares), in_specs=[smem, hbm, hbm,...  52.1 us
    pallas_call x1, Pallas kernels, local(): pl.pallas_call(write_kernel, out_shape=(dq, grads, grads), in_specs=[hbm,...  2.33 us

profile of v6, /device:TPU:8, one launch (start us, length us, event | category | flops | bytes accessed | tf_op | source)
XLA Modules:
  0.0 55.0 jit_solution(8624108484293453521)
XLA Ops:
  0.6 52.1 %attention_backward.1 = (bf16[2,192,512]{2,1,0:T(8,128)(2,1)}, bf16[4,4,4,48,128]{4,3,2,1,0:T(8,128)(2,1)}) custom-call(s32[32]{0:T(128)} %off_ref.1, bf16[2,192,512]{2,1,0:T(8,128)(2,1)} %q_ref.1, bf16[2,192,512]{2,1,0:T(8,128)(2,1)} %g_ref.1, bf16[2,96,1024]{2,1,0:T(8,128)(2,1)} %bitcast.2, bf16[2,96,1024]{2,1,0:T(8,128)(2,1)} %bitcast.3), custom_call_target="tpu_custom_call" | custom-call | flops 3400000000 | bytes 6000000 | tf_op jit(solution)/shard_map/attention_backward/pallas_call | solution.py:384
  52.7 2.3 %write_out.1 = (bf16[2,192,512]{2,1,0:T(8,128)(2,1)}, f32[192,1024]{1,0:T(8,128)}, f32[192,1024]{1,0:T(8,128)}) custom-call(bf16[2,192,512]{2,1,0:T(8,128)(2,1)} %get-tuple-element.5.dq_in, bf16[4,4,4,48,128]{4,3,2,1,0:T(8,128)(2,1)} %get-tuple-element.6.share_in), custom_call_target="tpu_custom_call" | custom-call | tf_op jit(solution)/shard_map/write_out/pallas_call | solution.py:408
